TPU v7x, 32 devices: a whole 2x2x4 slice. The times are simulated.
32 devices in a mesh: dp: 32 (over z, y, x, core).
Axes of the slice: x: 2, y: 2, z: 4, core: 2. Of those that a mesh axis runs over, the one named last changes fastest.
Arguments:
- query_tokens: bfloat16 [1024, 768], P('dp'), may hold values from -6 to 6
- passage_tokens: bfloat16 [14080, 768], P('dp'), may hold values from -6 to 6
- query_lengths: int32 [32], P('dp'), may hold values from 5 to 32, as said below
- passage_lengths: int32 [64], P('dp'), may hold values from 28 to 220, as said below
- passage_valid: int32 [64], P('dp'), may hold values 0 or 1
- positives: int32 [32], P('dp'), may hold values from 0 to 63
- negatives: int32 [32], P('dp'), may hold values from 0 to 63
- teacher_margins: float32 [32], P('dp'), may hold values from -8 to 8
- query_grad: bfloat16 [1024, 768], P('dp'), may hold values from -6 to 6
- passage_grad: bfloat16 [14080, 768], P('dp'), may hold values from -6 to 6
- weight_query: bfloat16 [768, 768], replicated, may hold values from -0.21875 to 0.21875
- bias_query: bfloat16 [768], replicated, may hold values from -1.75 to 1.75
- weight_key: bfloat16 [768, 768], replicated, may hold values from -0.21875 to 0.21875
- weight_value: bfloat16 [768, 768], replicated, may hold values from -0.21875 to 0.21875
- bias_value: bfloat16 [768], replicated, may hold values from -0.625 to 0.625
- weight_out: bfloat16 [768, 768], replicated, may hold values from -1.25 to 1.25
- bias_out: bfloat16 [768], replicated, may hold values from -1.75 to 1.75
- gain_attn: bfloat16 [768], replicated, may hold values from 0.5 to 1.5
- shift_attn: bfloat16 [768], replicated, may hold values from -1.25 to 1.25
- weight_in: bfloat16 [768, 3072], replicated, may hold values from -0.21875 to 0.21875
- bias_in: bfloat16 [3072], replicated, may hold values from -1.75 to 1.75
- weight_back: bfloat16 [3072, 768], replicated, may hold values from -0.109375 to 0.109375
- bias_back: bfloat16 [768], replicated, may hold values from -1.75 to 1.75
- gain_ffn: bfloat16 [768], replicated, may hold values from 0.5 to 1.5
- shift_ffn: bfloat16 [768], replicated, may hold values from -1.25 to 1.25
Outputs:
- query_out: bfloat16 [1024, 768], P('dp')
- passage_out: bfloat16 [14080, 768], P('dp')
- query_loss: float32 [32], P('dp')
- query_tokens_grad: float32 [1024, 768], P('dp')
- passage_tokens_grad: float32 [14080, 768], P('dp')
- weight_query_grad: float32 [768, 768], P('dp')
- bias_query_grad: float32 [768], P('dp')
- weight_key_grad: float32 [768, 768], P('dp')
- weight_value_grad: float32 [768, 768], P('dp')
- bias_value_grad: float32 [768], P('dp')
- weight_out_grad: float32 [768, 768], P('dp')
- bias_out_grad: float32 [768], P('dp')
- gain_attn_grad: float32 [768], P('dp')
- shift_attn_grad: float32 [768], P('dp')
- weight_in_grad: float32 [768, 3072], P('dp')
- bias_in_grad: float32 [3072], P('dp')
- weight_back_grad: float32 [3072, 768], P('dp')
- bias_back_grad: float32 [768], P('dp')
- gain_ffn_grad: float32 [768], P('dp')
- shift_ffn_grad: float32 [768], P('dp')
Inputs may be any that keep to these rules, and one draw needn't show every extreme that they name: `query_lengths`: some query slot in every draw uses all 32 tokens. `passage_lengths`: some passage slot in every draw uses all 220 tokens.
All inputs are finite; a program needn't handle non-finite values. No bound on the sum of `passage_valid` on one device may be relied on, other than what follows from the above.
Results may differ from a plain program's by a relative error of at most 0.014.
Values may be sent and summed in bfloat16 or wider, within the bound.
A program may use at most 192 MiB of HBM per device.

v0:
```python
import jax
import jax.numpy as jnp
from jax import lax
from jax.sharding import PartitionSpec as P

D = 768
HEADS = 12
HEAD_DIM = 64


ln_eps = 1e-12
score_scale = 0.0625
margin_weight = 0.5
root_half = 0.7071067811865476
inv_root_tau = 0.3989422804014327


def matmul(left, right):
    return jnp.dot(left, right, preferred_element_type=jnp.float32)


def left_across(left, right):
    return lax.dot_general(
        left, right, (((0,), (0,)), ((), ())), preferred_element_type=jnp.float32
    )


def right_across(left, right):
    return lax.dot_general(
        left, right, (((1,), (1,)), ((), ())), preferred_element_type=jnp.float32
    )


def normalize(hidden, gain, shift):
    centered = hidden - jnp.mean(hidden, axis=-1, keepdims=True)
    inv_std = lax.rsqrt(jnp.mean(centered * centered, axis=-1, keepdims=True) + ln_eps)
    unit_rows = centered * inv_std
    return (unit_rows * gain.astype(jnp.float32) + shift.astype(jnp.float32), unit_rows, inv_std)


def normalize_back(upstream, unit_rows, inv_std, gain):
    scaled = upstream * gain.astype(jnp.float32)
    hidden_grad = inv_std * (
        scaled
        - jnp.mean(scaled, axis=-1, keepdims=True)
        - unit_rows * jnp.mean(scaled * unit_rows, axis=-1, keepdims=True)
    )
    return (hidden_grad, jnp.sum(upstream * unit_rows, axis=0), jnp.sum(upstream, axis=0))


def gelu_exact(inputs):
    return 0.5 * inputs * (1.0 + lax.erf(inputs * root_half))


def gelu_slope(inputs):
    return 0.5 * (1.0 + lax.erf(inputs * root_half)) + inputs * inv_root_tau * jnp.exp(
        -0.5 * inputs * inputs
    )


def head_scores(query_heads, key_heads, lengths):
    slot_length = query_heads.shape[1]
    allowed = (lax.iota(jnp.int32, slot_length)[None, :] < lengths[:, None])[:, None, None, :]
    raw_scores = 0.125 * jnp.einsum(
        "bqhd,bkhd->bhqk", query_heads, key_heads, preferred_element_type=jnp.float32
    )
    return jnp.where(allowed, raw_scores, -1000000000.0)


def encode_forward(tokens, lengths, params):
    (
        weight_query,
        bias_query,
        weight_key,
        weight_value,
        bias_value,
        weight_out,
        bias_out,
        gain_attn,
        shift_attn,
        weight_in,
        bias_in,
        weight_back,
        bias_back,
        gain_ffn,
        shift_ffn,
    ) = params
    slot_count = lengths.shape[0]
    row_count = tokens.shape[0]
    split_heads = (slot_count, row_count // slot_count, HEADS, HEAD_DIM)
    queries = (matmul(tokens, weight_query) + bias_query.astype(jnp.float32)).astype(jnp.bfloat16)
    keys_all = matmul(tokens, weight_key).astype(jnp.bfloat16)
    values_all = (matmul(tokens, weight_value) + bias_value.astype(jnp.float32)).astype(
        jnp.bfloat16
    )
    scores = head_scores(queries.reshape(split_heads), keys_all.reshape(split_heads), lengths)
    peak_score = jnp.max(scores, axis=-1, keepdims=True)
    exp_scores = jnp.exp(scores - peak_score)
    row_total = jnp.sum(exp_scores, axis=-1, keepdims=True)
    soft_low = (exp_scores / row_total).astype(jnp.bfloat16)
    log_total = peak_score + jnp.log(row_total)
    context = jnp.einsum(
        "bhqk,bkhd->bqhd",
        soft_low,
        values_all.reshape(split_heads),
        preferred_element_type=jnp.float32,
    )
    context = context.reshape(row_count, D).astype(jnp.bfloat16)
    attn_sum = (
        tokens.astype(jnp.float32) + matmul(context, weight_out) + bias_out.astype(jnp.float32)
    )
    middle, unit_attn, inv_attn = normalize(attn_sum, gain_attn, shift_attn)
    middle_low = middle.astype(jnp.bfloat16)
    inner_act = matmul(middle_low, weight_in) + bias_in.astype(jnp.float32)
    gelu_low = gelu_exact(inner_act).astype(jnp.bfloat16)
    ffn_sum = middle + matmul(gelu_low, weight_back) + bias_back.astype(jnp.float32)
    output, unit_ffn, inv_ffn = normalize(ffn_sum, gain_ffn, shift_ffn)
    kept = (
        queries,
        keys_all,
        values_all,
        log_total,
        context,
        unit_attn,
        inv_attn,
        middle_low,
        inner_act,
        gelu_low,
        unit_ffn,
        inv_ffn,
    )
    return (output.astype(jnp.bfloat16), kept)


def ffn_backward(upstream, kept, params):
    (
        queries,
        keys_all,
        values_all,
        log_total,
        context,
        unit_attn,
        inv_attn,
        middle_low,
        inner_act,
        gelu_low,
        unit_ffn,
        inv_ffn,
    ) = kept
    weight_in, weight_back, gain_ffn = (params[9], params[11], params[13])
    ffn_grad, gain_grad, shift_grad = normalize_back(upstream, unit_ffn, inv_ffn, gain_ffn)
    branch_low = ffn_grad.astype(jnp.bfloat16)
    back_weight_grad = left_across(gelu_low, branch_low)
    back_bias_grad = jnp.sum(branch_low, axis=0, dtype=jnp.float32)
    inner_low = (right_across(branch_low, weight_back) * gelu_slope(inner_act)).astype(jnp.bfloat16)
    in_weight_grad = left_across(middle_low, inner_low)
    in_bias_grad = jnp.sum(inner_low, axis=0, dtype=jnp.float32)
    middle_grad = ffn_grad + right_across(inner_low, weight_in)
    return (
        middle_grad,
        (in_weight_grad, in_bias_grad, back_weight_grad, back_bias_grad, gain_grad, shift_grad),
    )


def attention_backward(middle_grad, tokens, lengths, kept, params):
    (
        queries,
        keys_all,
        values_all,
        log_total,
        context,
        unit_attn,
        inv_attn,
        middle_low,
        inner_act,
        gelu_low,
        unit_ffn,
        inv_ffn,
    ) = kept
    weight_query, weight_key, weight_value, weight_out, gain_attn = (
        params[0],
        params[2],
        params[3],
        params[5],
        params[7],
    )
    slot_count = lengths.shape[0]
    row_count = tokens.shape[0]
    split_heads = (slot_count, row_count // slot_count, HEADS, HEAD_DIM)
    attn_grad, gain_grad, shift_grad = normalize_back(middle_grad, unit_attn, inv_attn, gain_attn)
    attn_low = attn_grad.astype(jnp.bfloat16)
    out_weight_grad = left_across(context, attn_low)
    out_bias_grad = jnp.sum(attn_low, axis=0, dtype=jnp.float32)
    context_grad = right_across(attn_low, weight_out).astype(jnp.bfloat16).reshape(split_heads)
    query_heads = queries.reshape(split_heads)
    key_heads = keys_all.reshape(split_heads)
    value_heads = values_all.reshape(split_heads)
    soft_full = jnp.exp(head_scores(query_heads, key_heads, lengths) - log_total)
    soft_grad = jnp.einsum(
        "bqhd,bkhd->bhqk", context_grad, value_heads, preferred_element_type=jnp.float32
    )
    value_grad = jnp.einsum(
        "bhqk,bqhd->bkhd",
        soft_full.astype(jnp.bfloat16),
        context_grad,
        preferred_element_type=jnp.float32,
    )
    value_grad = value_grad.reshape(row_count, D).astype(jnp.bfloat16)
    score_low = (
        soft_full * (soft_grad - jnp.sum(soft_full * soft_grad, axis=-1, keepdims=True))
    ).astype(jnp.bfloat16)
    query_grad_low = 0.125 * jnp.einsum(
        "bhqk,bkhd->bqhd", score_low, key_heads, preferred_element_type=jnp.float32
    )
    query_grad_low = query_grad_low.reshape(row_count, D).astype(jnp.bfloat16)
    key_grad_low = 0.125 * jnp.einsum(
        "bhqk,bqhd->bkhd", score_low, query_heads, preferred_element_type=jnp.float32
    )
    key_grad_low = key_grad_low.reshape(row_count, D).astype(jnp.bfloat16)
    token_grad = (
        attn_grad
        + right_across(query_grad_low, weight_query)
        + right_across(key_grad_low, weight_key)
        + right_across(value_grad, weight_value)
    )
    grads = (
        left_across(tokens, query_grad_low),
        jnp.sum(query_grad_low, axis=0, dtype=jnp.float32),
        left_across(tokens, key_grad_low),
        left_across(tokens, value_grad),
        jnp.sum(value_grad, axis=0, dtype=jnp.float32),
        out_weight_grad,
        out_bias_grad,
        gain_grad,
        shift_grad,
    )
    return (token_grad, grads)


def on_device(
    query_tokens,
    passage_tokens,
    query_lengths,
    passage_lengths,
    passage_valid,
    positives,
    negatives,
    teacher_margins,
    query_grad,
    passage_grad,
    weight_query,
    bias_query,
    weight_key,
    weight_value,
    bias_value,
    weight_out,
    bias_out,
    gain_attn,
    shift_attn,
    weight_in,
    bias_in,
    weight_back,
    bias_back,
    gain_ffn,
    shift_ffn,
):
    params = (
        weight_query,
        bias_query,
        weight_key,
        weight_value,
        bias_value,
        weight_out,
        bias_out,
        gain_attn,
        shift_attn,
        weight_in,
        bias_in,
        weight_back,
        bias_back,
        gain_ffn,
        shift_ffn,
    )
    query_out, query_kept = encode_forward(query_tokens, query_lengths, params)
    passage_out, passage_kept = encode_forward(passage_tokens, passage_lengths, params)
    query_slots = query_lengths.shape[0]
    passage_slots = passage_lengths.shape[0]
    cls_query = query_out.reshape(query_slots, -1, D)[:, 0]
    cls_passage = passage_out.reshape(passage_slots, -1, D)[:, 0]
    valid_low = passage_valid.astype(jnp.bfloat16)

    def score_piece(cls_piece, valid_piece):
        scores = score_scale * right_across(cls_query, cls_piece)
        position = lax.iota(jnp.int32, cls_piece.shape[0])
        is_positive = position[None, :] == positives[:, None]
        is_negative = position[None, :] == negatives[:, None]
        allowed = (valid_piece[None, :] > 0.5) | is_positive
        return (scores, allowed, is_positive, is_negative)

    peak_score = jnp.full((query_slots,), -1e30, jnp.float32)
    scores, allowed, is_positive, is_negative = score_piece(
        lax.all_gather(cls_passage, "dp", axis=0, tiled=True),
        lax.all_gather(valid_low, "dp", axis=0, tiled=True),
    )
    masked = jnp.where(allowed, scores, -1e30)
    new_peak = jnp.maximum(peak_score, jnp.max(masked, axis=1))
    row_total = jnp.sum(jnp.where(allowed, jnp.exp(masked - new_peak[:, None]), 0.0), axis=1)
    positive_score = jnp.sum(jnp.where(is_positive, scores, 0.0), axis=1)
    negative_score = jnp.sum(jnp.where(is_negative, scores, 0.0), axis=1)
    peak_score, row_total, positive_score, negative_score = (
        new_peak,
        row_total,
        positive_score,
        negative_score,
    )
    all_cls, all_valid = (
        lax.all_gather(cls_passage, "dp", axis=0, tiled=True),
        lax.all_gather(valid_low, "dp", axis=0, tiled=True),
    )
    log_total = peak_score + jnp.log(row_total)
    shortfall = positive_score - negative_score - teacher_margins
    query_loss = log_total - positive_score + margin_weight * shortfall * shortfall
    scores, allowed, is_positive, is_negative = score_piece(all_cls, all_valid)
    soft_scores = jnp.where(allowed, jnp.exp(scores - log_total[:, None]), 0.0)
    positive_hit = is_positive.astype(jnp.float32)
    negative_hit = is_negative.astype(jnp.float32)
    score_grad = (
        soft_scores
        - positive_hit
        + 2.0 * margin_weight * shortfall[:, None] * (positive_hit - negative_hit)
    ).astype(jnp.bfloat16)
    cls_query_grad = score_scale * matmul(score_grad, all_cls)
    cls_passage_grad = lax.psum_scatter(
        score_scale * left_across(score_grad, cls_query), "dp", scatter_dimension=0, tiled=True
    )
    query_upstream = (
        query_grad.astype(jnp.float32)
        .reshape(query_slots, -1, D)
        .at[:, 0]
        .add(cls_query_grad)
        .reshape(-1, D)
    )
    passage_upstream = (
        passage_grad.astype(jnp.float32)
        .reshape(passage_slots, -1, D)
        .at[:, 0]
        .add(cls_passage_grad)
        .reshape(-1, D)
    )
    query_middle_grad, query_ffn = ffn_backward(query_upstream, query_kept, params)
    passage_middle_grad, passage_ffn = ffn_backward(passage_upstream, passage_kept, params)
    (
        in_weight_grad,
        in_bias_grad,
        back_weight_grad,
        back_bias_grad,
        ffn_gain_grad,
        ffn_shift_grad,
    ) = tuple((first + second for first, second in zip(query_ffn, passage_ffn)))
    query_tokens_grad, query_attn = attention_backward(
        query_middle_grad, query_tokens, query_lengths, query_kept, params
    )
    passage_tokens_grad, passage_attn = attention_backward(
        passage_middle_grad, passage_tokens, passage_lengths, passage_kept, params
    )
    (
        query_weight_grad,
        query_bias_grad,
        key_weight_grad,
        value_weight_grad,
        value_bias_grad,
        out_weight_grad,
        out_bias_grad,
        attn_gain_grad,
        attn_shift_grad,
    ) = tuple((first + second for first, second in zip(query_attn, passage_attn)))
    (
        query_weight_grad,
        query_bias_grad,
        key_weight_grad,
        value_weight_grad,
        value_bias_grad,
        out_weight_grad,
        out_bias_grad,
        attn_gain_grad,
        attn_shift_grad,
        in_weight_grad,
        in_bias_grad,
        back_weight_grad,
        back_bias_grad,
        ffn_gain_grad,
        ffn_shift_grad,
    ) = (
        lax.psum_scatter(query_weight_grad, "dp", scatter_dimension=0, tiled=True),
        lax.psum_scatter(query_bias_grad, "dp", scatter_dimension=0, tiled=True),
        lax.psum_scatter(key_weight_grad, "dp", scatter_dimension=0, tiled=True),
        lax.psum_scatter(value_weight_grad, "dp", scatter_dimension=0, tiled=True),
        lax.psum_scatter(value_bias_grad, "dp", scatter_dimension=0, tiled=True),
        lax.psum_scatter(out_weight_grad, "dp", scatter_dimension=0, tiled=True),
        lax.psum_scatter(out_bias_grad, "dp", scatter_dimension=0, tiled=True),
        lax.psum_scatter(attn_gain_grad, "dp", scatter_dimension=0, tiled=True),
        lax.psum_scatter(attn_shift_grad, "dp", scatter_dimension=0, tiled=True),
        lax.psum_scatter(in_weight_grad, "dp", scatter_dimension=0, tiled=True),
        lax.psum_scatter(in_bias_grad, "dp", scatter_dimension=0, tiled=True),
        lax.psum_scatter(back_weight_grad, "dp", scatter_dimension=0, tiled=True),
        lax.psum_scatter(back_bias_grad, "dp", scatter_dimension=0, tiled=True),
        lax.psum_scatter(ffn_gain_grad, "dp", scatter_dimension=0, tiled=True),
        lax.psum_scatter(ffn_shift_grad, "dp", scatter_dimension=0, tiled=True),
    )
    return (
        query_out,
        passage_out,
        query_loss,
        query_tokens_grad,
        passage_tokens_grad,
        query_weight_grad,
        query_bias_grad,
        key_weight_grad,
        value_weight_grad,
        value_bias_grad,
        out_weight_grad,
        out_bias_grad,
        attn_gain_grad,
        attn_shift_grad,
        in_weight_grad,
        in_bias_grad,
        back_weight_grad,
        back_bias_grad,
        ffn_gain_grad,
        ffn_shift_grad,
    )


def solution(mesh):
    return jax.shard_map(
        on_device,
        mesh=mesh,
        in_specs=(
            P("dp", None),
            P("dp", None),
            P("dp"),
            P("dp"),
            P("dp"),
            P("dp"),
            P("dp"),
            P("dp"),
            P("dp", None),
            P("dp", None),
            P(),
            P(),
            P(),
            P(),
            P(),
            P(),
            P(),
            P(),
            P(),
            P(),
            P(),
            P(),
            P(),
            P(),
            P(),
        ),
        out_specs=(
            P("dp", None),
            P("dp", None),
            P("dp"),
            P("dp", None),
            P("dp", None),
            P("dp", None),
            P("dp"),
            P("dp", None),
            P("dp", None),
            P("dp"),
            P("dp", None),
            P("dp"),
            P("dp"),
            P("dp"),
            P("dp", None),
            P("dp"),
            P("dp", None),
            P("dp"),
            P("dp"),
            P("dp"),
        ),
        check_vma=False,
    )
```

profile of v0, /device:TPU:0, one launch (start us, length us, event | category | flops | bytes accessed | tf_op | source)
XLA Modules:
  0.0 1033.7 jit_solution(16813359990217027287)
XLA Ops:
  10.4 3.2 fusion.18
  20.9 3.3 convolution_add_fusion.2
  24.3 3.5 fusion.86
  28.9 2.8 reshape.501
  33.8 2.5 reshape.502
  38.4 2.5 reshape.503
  43.7 2.8 fusion.87
  51.7 3.2 convert_element_type.308
  54.9 2.1 fusion.88
  57.9 6.1 multiply_convert_fusion.1
  64.0 2.5 fusion.89
  68.1 42.1 %all-reduce = bf16[64]{0:T(256)(128)(2,1)S(1)} all-reduce(bf16[64]{0:T(256)(128)(2,1)S(1)} %dynamic-update-slice.7), channel_id=1, replica_groups=mesh['dp'=32] {'dp'}, use_global_device_ids=true, to_apply=%add | all-reduce | flops 64 | bytes 256
  111.3 2.1 reshape.477
  114.2 40.7 %all-gather = bf16[64,1,768]{2,1,0:T(2,128)(2,1)S(1)} all-gather(bf16[2,1,768]{2,1,0:T(2,128)(2,1)S(1)} %slice.55), channel_id=2, replica_groups=mesh['dp'=32] {'dp'}, dimensions={0}, use_global_device_ids=true | all-gather | bytes 101376 | tf_op jit(solution)/shard_map/all_gather | solution.py:302
  165.0 4.5 convert_reduce_fusion.5
  170.2 4.5 multiply_reduce_fusion.11
  179.8 2.3 reshape.486
  182.1 98.3 %all-reduce.14.cloned.1.call-done = f32[64,768]{1,0:T(8,128)} async-done(((f32[64,768]{1,0:T(8,128)}), f32[64,768]{1,0:T(8,128)}) %all-reduce.14.cloned.1.call-update) | async-done | bytes 196624
  283.4 2.6 reshape.483
  286.0 2.2 fusion.81
  289.4 2.5 convert_reduce_fusion.3
  291.9 7.8 convert_reduce_fusion
  299.7 3.3 multiply_reduce_fusion.3
  305.9 2.3 reshape.504
  308.1 2.5 copy.130
  310.7 4.3 multiply_reduce_fusion
  319.8 2.7 convert_element_type.342
  322.5 3.6 add_bitcast_fusion.2
  326.1 3.1 copy.150
  331.5 2.7 fusion.21
  335.9 2.5 convert_element_type.345
  338.5 3.6 add_bitcast_fusion.1
  342.1 3.1 copy.152
  348.1 3.7 convert_reduce_fusion.1
  353.5 2.5 convert_element_type.349
  356.1 3.6 add_bitcast_fusion
  359.6 3.1 copy.154
  364.5 2.2 convolution_add_fusion.3
  367.4 5.1 fusion.77
  372.5 5.2 convolution_add_fusion.1
  377.8 5.1 fusion.67
  382.9 5.1 convolution_add_fusion
  392.5 42.1 %all-reduce.11 = (f32[768]{0:T(1024)S(1)}, f32[768]{0:T(1024)S(1)}, f32[768]{0:T(1024)S(1)}, f32[768]{0:T(1024)S(1)}, f32[768]{0:T(1024)S(1)}, /*index=5*/f32[30...) all-reduce(f32[768]{0:T(1024)S(1)} %add.388, ...), channel_id=5, replica_groups=mesh['dp'=32] {'dp'}, use_global_device_ids=true, to_apply=%region_30.31.clone | all-reduce | flops 9216 | bytes 73728
  444.9 89.3 %reduce-scatter.21.cloned.1.call-done = f32[24,768]{1,0:T(8,128)} async-done(((f32[768,768]{1,0:T(8,128)}), f32[24,768]{1,0:T(8,128)}) %reduce-scatter.21.cloned.1.call-update) | async-done | bytes 73744
  534.1 103.8 %reduce-scatter.23.cloned.1.call-done = f32[24,768]{1,0:T(8,128)} async-done(((f32[768,768]{1,0:T(8,128)}), f32[24,768]{1,0:T(8,128)}) %reduce-scatter.23.cloned.1.call-update) | async-done | bytes 73744
  637.9 104.6 %reduce-scatter.13.cloned.1.call-done = f32[24,768]{1,0:T(8,128)} async-done(((f32[768,768]{1,0:T(8,128)}), f32[24,768]{1,0:T(8,128)}) %reduce-scatter.13.cloned.1.call-update) | async-done | bytes 73744 | tf_op jit(solution)/shard_map/reduce_scatter | solution.py:399
  742.5 140.9 %reduce-scatter.15.cloned.1.call-done = f32[24,3072]{1,0:T(8,128)} async-done(((f32[768,3072]{1,0:T(8,128)}), f32[24,3072]{1,0:T(8,128)}) %reduce-scatter.15.cloned.1.call-update) | async-done | bytes 294928 | tf_op jit(solution)/shard_map/reduce_scatter | solution.py:403
  883.4 142.1 %reduce-scatter.17.cloned.1.call-done = f32[96,768]{1,0:T(8,128)} async-done(((f32[3072,768]{1,0:T(8,128)}), f32[96,768]{1,0:T(8,128)}) %reduce-scatter.17.cloned.1.call-update) | async-done | bytes 294928 | tf_op jit(solution)/shard_map/reduce_scatter | solution.py:405
  (422 shorter events, 74.5 us)
Async XLA Ops:
  7.2 13.0 %copy-start = (bf16[768,768]{1,0:T(8,128)(2,1)S(1)}, bf16[768,768]{1,0:T(8,128)(2,1)}, u32[]{:S(2)}) copy-start(bf16[768,768]{1,0:T(8,128)(2,1)} %param.44) | copy-start | bytes 3538948
  7.2 273.2 %all-reduce.14.cloned.1.call-start = ((), (), s32[]{:S(2)}) async-start(), calls=%async_computation.12 | async-start | bytes 393216
  20.1 43.8 %copy-start.77 = (f32[768]{0:T(1024)}, f32[768]{0:T(1024)S(1)}, u32[]{:S(2)}) copy-start(f32[768]{0:T(1024)S(1)} %convert_element_type.293) | copy-start | bytes 9220
  20.6 154.1 %copy-start.31 = (f32[32,768]{1,0:T(8,128)}, f32[32,768]{1,0:T(8,128)S(1)}, u32[]{:S(2)}) copy-start(f32[32,768]{1,0:T(8,128)S(1)} %get-tuple-element.145) | copy-start | bytes 294916
  20.9 134.0 %copy-start.75 = (f32[768]{0:T(1024)}, f32[768]{0:T(1024)S(1)}, u32[]{:S(2)}) copy-start(f32[768]{0:T(1024)S(1)} %convert_element_type.299) | copy-start | bytes 9220
  24.3 140.7 %copy-start.25 = (f32[32,3072]{1,0:T(8,128)}, f32[32,3072]{1,0:T(8,128)S(1)}, u32[]{:S(2)}) copy-start(f32[32,3072]{1,0:T(8,128)S(1)} %convolution_add_fusion.2) | copy-start | bytes 1179652
  50.0 5.0 copy-start.28
  51.7 5.7 slice-start.4
  57.1 6.9 copy-start.29
  57.1 6.9 copy-start.90
  57.1 6.9 slice-start.2
  57.8 6.1 copy-start.115
  57.9 6.1 slice-start.3
  67.2 46.2 %copy-start.88 = (f32[440]{0:T(512)}, f32[440]{0:T(512)S(1)}, u32[]{:S(2)}) copy-start(f32[440]{0:T(512)S(1)} %add_rsqrt_fusion) | copy-start | bytes 5284
  110.2 44.7 %copy-start.34 = (f32[32,768]{1,0:T(8,128)S(1)}, f32[32,768]{1,0:T(8,128)}, u32[]{:S(2)}) copy-start(f32[32,768]{1,0:T(8,128)} %copy-done.33) | copy-start | bytes 294916
  110.2 44.7 %copy-start.107 = (f32[32]{0:T(128)S(1)}, f32[32]{0:T(128)}, u32[]{:S(2)}) copy-start(f32[32]{0:T(128)} %copy-done.106) | copy-start | bytes 388
  110.2 44.7 %copy-start.113 = (f32[32]{0:T(128)S(1)}, f32[32]{0:T(128)}, u32[]{:S(2)}) copy-start(f32[32]{0:T(128)} %add_rsqrt_fusion.2) | copy-start | bytes 388
  111.3 49.9 %copy-start.87 = (f32[12,32]{1,0:T(8,128)S(1)}, f32[12,32]{1,0:T(8,128)}, u32[]{:S(2)}) copy-start(f32[12,32]{1,0:T(8,128)} %copy-done.86) | copy-start | bytes 4612
  161.1 283.8 %reduce-scatter.19.cloned.1.call-start = ((), (), s32[]{:S(2)}) async-start(), calls=%async_computation.9 | async-start | bytes 2433024
  165.0 4.5 copy-start.46
  165.0 5.2 copy-start.94
  165.0 5.2 copy-start.110
  177.8 4.3 copy-start.59
  179.8 135.3 %copy-start.55 = (f32[2,12,220]{2,1,0:T(8,128)}, f32[2,12,220]{2,1,0:T(8,128)S(1)}, u32[]{:S(2)}) copy-start(f32[2,12,220]{2,1,0:T(8,128)S(1)} %log_add_fusion) | copy-start | bytes 63364
  289.4 10.3 slice-start.6
  291.9 7.8 copy-start.50
  291.9 7.8 slice-start.7
  291.9 7.8 copy-start.30
  291.9 7.8 copy-start.91
  291.9 7.8 copy-start.116
  308.1 6.9 slice-start
  310.6 4.4 copy-start.21
  310.7 4.4 slice-start.1
  318.1 4.4 copy-start.14
  329.2 205.0 %reduce-scatter.21.cloned.1.call-start = ((), (), s32[]{:S(2)}) async-start(), calls=%async_computation.10 | async-start | bytes 2433024
  345.2 292.7 %reduce-scatter.23.cloned.1.call-start = ((), (), s32[]{:S(2)}) async-start(), calls=%async_computation.11 | async-start | bytes 2433024
  347.1 4.7 copy-start.63
  362.8 379.7 %reduce-scatter.13.cloned.1.call-start = ((), (), s32[]{:S(2)}) async-start(), calls=%async_computation.6 | async-start | bytes 2433024 | tf_op jit(solution)/shard_map/reduce_scatter | solution.py:399
  366.7 5.8 copy-start.32
  366.7 5.8 copy-start.45
  366.7 5.8 copy-start.95
  366.7 5.8 copy-start.111
  366.7 516.7 %reduce-scatter.15.cloned.1.call-start = ((), (), s32[]{:S(2)}) async-start(), calls=%async_computation.7 | async-start | bytes 9732096 | tf_op jit(solution)/shard_map/reduce_scatter | solution.py:403
  377.7 5.2 copy-start.26
  377.7 5.2 copy-start.47
  377.7 647.8 %reduce-scatter.17.cloned.1.call-start = ((), (), s32[]{:S(2)}) async-start(), calls=%async_computation.8 | async-start | bytes 9732096 | tf_op jit(solution)/shard_map/reduce_scatter | solution.py:405
  390.4 49.5 %copy-start.16 = (bf16[440,768]{0,1:T(8,128)(2,1)S(1)}, bf16[440,768]{0,1:T(8,128)(2,1)}, u32[]{:S(2)}) copy-start(bf16[440,768]{0,1:T(8,128)(2,1)} %copy-done.15) | copy-start | bytes 2027524
  441.4 584.1 %copy-start.1 = (bf16[768,768]{1,0:T(8,128)(2,1)S(1)}, bf16[768,768]{1,0:T(8,128)(2,1)}, u32[]{:S(2)}) copy-start(bf16[768,768]{1,0:T(8,128)(2,1)} %param.44) | copy-start | bytes 3538948
  (97 other events, 178.8 us)
Sparse Core Ops, SparseCore 0:
  161.2 119.1 all-reduce.13
  329.3 99.9 reduce-scatter.18
  436.0 98.0 reduce-scatter.20
  539.8 97.9 reduce-scatter.22
  644.5 97.9 reduce-scatter.12
  748.8 134.5 reduce-scatter.14
  890.9 134.6 reduce-scatter.16
where the time goes:
time: 1040 us; the launch traced here: 1030 us
  waiting for transfers between devices  679 us (65%)
  blocking collectives  125 us (12%)
  matrix products  110 us (11%)
  local copies, waits for them, and re-layouts  74.9 us (7%)
  between operations  23.1 us (2%)
  other arithmetic  21.4 us (2%)
    unnamed x11, waiting for transfers between devices  291 us
    reduce_scatter x1, waiting for transfers between devices, on_device(): lax.psum_scatter(back_weight_grad, 'dp', scatter_dimension=0, tiled=True)  142 us
    reduce_scatter x1, waiting for transfers between devices, on_device(): lax.psum_scatter(in_weight_grad, 'dp', scatter_dimension=0, tiled=True)  141 us
    reduce_scatter x1, waiting for transfers between devices, on_device(): lax.psum_scatter(out_weight_grad, 'dp', scatter_dimension=0, tiled=True)  105 us
    unnamed x2, blocking collectives  84.2 us
    all_gather x1, blocking collectives, on_device(): lax.all_gather(cls_passage, 'dp', axis=0, tiled=True)  40.7 us
    dot_general x12, matrix products, left_across(): lax.dot_general(left, right, (((0,), (0,)), ((), ())), preferred_element_...  36.8 us
    dot_general x13, matrix products, right_across(): lax.dot_general(left, right, (((1,), (1,)), ((), ())), preferred_element_...  27.6 us
  transfers between devices with their start and end apart: 7, of which 6 were waited for; matrix products, arithmetic and copies ran while one was open for 8% of the time, Pallas kernels for 0%

commit v1 on v0

--- a/solution.py
+++ b/solution.py
@@ -1,6 +1,8 @@
 import jax
 import jax.numpy as jnp
 from jax import lax
+from jax.experimental import pallas as pl
+from jax.experimental.pallas import tpu as pltpu
 from jax.sharding import PartitionSpec as P
 
 D = 768
@@ -431,9 +433,683 @@
     )
 
 
+F32 = jnp.float32
+BF16 = jnp.bfloat16
+MESH = pl.DeviceIdType.MESH
+FF = 3072
+ROWS = 480
+WIN = 240
+SLOT = 220
+NEG = -1000000000.0
+
+
+def dot_nn(left, right):
+    return jnp.dot(left, right, preferred_element_type=F32)
+
+
+def dot_nt(left, right):
+    return lax.dot_general(left, right, (((1,), (1,)), ((), ())), preferred_element_type=F32)
+
+
+def dot_tn(left, right):
+    return lax.dot_general(left, right, (((0,), (0,)), ((), ())), preferred_element_type=F32)
+
+
+def row_of(ref, start=0, size=D):
+    return ref[pl.ds(start, size)].astype(F32).reshape(1, size)
+
+
+def iota(shape, dim):
+    return lax.broadcasted_iota(jnp.int32, shape, dim)
+
+
+def fold8(block):
+    return jnp.sum(block.reshape(-1, 8, block.shape[-1]), axis=0)
+
+
+def layer_kernel(
+    qtok, ptok, qlen, plen, pvalid, pos, neg, margin, qgrad, pgrad,
+    wq_h, bq, wk_h, wv_h, bv, wo_h, bo, ga, sa, wi_h, bi, wb_h, bb, gf, sf,
+    qout_h, pout_h, loss_o, qtg_h, ptg_h, wqg, bqg, wkg, wvg, bvg, wog, bog, gag, sag,
+    wig, big, wbg, bbg, gfg, sfg,
+    wq, wk, wv, wo, wi, wb, pstage, x_s, xT, q_s, k_s, v_s, p_s, pq_s, c_s, cT, n1, n2, r1, r2,
+    ml, mlT, act_s, actT, tmp, gp, qg_s, pg_s, qo_s, po_s, ex, dcls, vec, vecr, vecz,
+    g_s, rc, ra, rb, rz,
+    load_sem, out_sem, ex_send, ex_recv, c_send, c_recv, a_send, a_recv, b_send, b_recv,
+    z_send, z_recv, v_send, v_recv, credit,
+):
+    me = lax.axis_index("dp")
+    core = lax.rem(me, 2)
+    xx = lax.rem(lax.div(me, 2), 2)
+    yy = lax.rem(lax.div(me, 4), 2)
+    zz = lax.div(me, 8)
+    chip = lax.div(me, 2)
+    partner = me + 1 - 2 * core
+    x_peer = me + 2 - 4 * xx
+    y_peer = me + 4 - 8 * yy
+    plane = lax.rem(me, 8)
+
+    loads = {}
+    for at, (name, source, target) in enumerate((
+        ("ptok", ptok, pstage), ("qtok", qtok, qo_s), ("wq", wq_h, wq), ("wk", wk_h, wk), ("wv", wv_h, wv),
+        ("wo", wo_h, wo), ("wi", wi_h, wi), ("wb", wb_h, wb), ("qg", qgrad, qg_s), ("pg", pgrad, pg_s),
+    )):
+        loads[name] = pltpu.make_async_copy(source, target, load_sem.at[at])
+        loads[name].start()
+
+    barrier = pltpu.get_barrier_semaphore()
+    for hop in range(1, 16):
+        other = 2 * lax.rem(chip + hop, 16) + core
+        pl.semaphore_signal(barrier, inc=1, device_id=(other,), device_id_type=MESH)
+    pl.semaphore_signal(barrier, inc=1, device_id=(partner,), device_id_type=MESH)
+
+    loads["ptok"].wait()
+    loads["qtok"].wait()
+    x_s[0:32, :] = qo_s[...]
+
+    def copy_tokens(i, carry):
+        x_s[pl.ds(pl.multiple_of(32 + i * 16, 16), 16), :] = pstage[pl.ds(pl.multiple_of(i * 16, 16), 16), :]
+        return carry
+
+    lax.fori_loop(0, 27, copy_tokens, 0)
+    x_s[464:480, :] = jnp.concatenate(
+        [pstage[432:440, :].astype(F32), jnp.zeros((8, D), F32)], axis=0
+    ).astype(BF16)
+
+    loads["wq"].wait()
+    q_s[...] = ((dot_nn(x_s[...], wq[...]) + row_of(bq)).astype(BF16) * 0.125).astype(BF16)
+    loads["wk"].wait()
+    k_s[...] = dot_nn(x_s[...], wk[...]).astype(BF16)
+    loads["wv"].wait()
+    v_s[...] = (dot_nn(x_s[...], wv[...]) + row_of(bv)).astype(BF16)
+
+    head_of = iota((12, 1, D), 2) // 64
+    head_mask = (head_of == iota((12, 1, D), 0)).astype(F32)
+
+    def spread(rows):
+        return (rows.astype(F32)[None] * head_mask).astype(BF16).reshape(384, D)
+
+    def gather_heads(stacked):
+        return jnp.sum(stacked.reshape(12, 32, D) * head_mask, axis=0)
+
+    raw = dot_nt(k_s[0:32, :], spread(q_s[0:32, :]))
+    raw = jnp.where(iota((32, 384), 0) < qlen[0], raw, NEG)
+    soft = jnp.exp(raw - jnp.max(raw, axis=0, keepdims=True))
+    soft = (soft * (1.0 / jnp.sum(soft, axis=0, keepdims=True))).astype(BF16)
+    pq_s[...] = soft
+    c_s[0:32, :] = gather_heads(dot_tn(soft, v_s[0:32, :])).astype(BF16)
+
+    lane = iota((1, 128), 1)
+    half = ((lane < 64).astype(BF16), (lane >= 64).astype(BF16))
+    key_at = iota((WIN, 1), 0)
+
+    def attend(pair, carry):
+        lanes = pl.ds(pl.multiple_of(pair * 128, 128), 128)
+        for slot in range(2):
+            low_at = 12 * slot
+            rows = pl.ds(32 + 208 * slot, WIN)
+            keys, queries = k_s[rows, lanes], q_s[rows, lanes]
+            values_t = v_s[rows, lanes].T
+            allowed = (key_at >= low_at) & (key_at < low_at + plen[slot])
+            parts = []
+            for h in range(2):
+                scores = jnp.where(allowed, dot_nt(keys, queries * half[h]), NEG)
+                e = jnp.exp(scores - jnp.max(scores, axis=0, keepdims=True))
+                p = (e * (1.0 / jnp.sum(e, axis=0, keepdims=True))).astype(BF16)
+                p_s[slot, 2 * pair + h] = p
+                parts.append(dot_nn(values_t, p)[64 * h:64 * h + 64, :])
+            context = jnp.concatenate(parts, axis=0).T
+            if slot == 0:
+                c_s[rows, lanes] = context.astype(BF16)
+            else:
+                old = c_s[240:256, lanes].astype(F32)
+                c_s[240:256, lanes] = jnp.where(iota((16, 128), 0) >= 12, context[0:16], old).astype(BF16)
+                c_s[256:480, lanes] = context[16:240].astype(BF16)
+        return carry
+
+    lax.fori_loop(0, 6, attend, 0)
+
+    loads["wo"].wait()
+    tmp[...] = dot_nn(c_s[...], wo[...])
+    gain1, shift1, bias1 = row_of(ga), row_of(sa), row_of(bo)
+
+    def norm_attn(i, carry):
+        rows = pl.ds(pl.multiple_of(i * 16, 16), 16)
+        hidden = tmp[rows, :] + x_s[rows, :].astype(F32) + bias1
+        centered = hidden - jnp.mean(hidden, axis=-1, keepdims=True)
+        inv = lax.rsqrt(jnp.mean(centered * centered, axis=-1, keepdims=True) + ln_eps)
+        unit = centered * inv
+        n1[rows, :] = unit
+        r1[rows, :] = inv
+        ml[rows, :] = (unit * gain1 + shift1).astype(BF16)
+        return carry
+
+    lax.fori_loop(0, 30, norm_attn, 0)
+
+    loads["wi"].wait()
+    loads["wb"].wait()
+
+    def wb_tile(t):
+        return wb[lax.div(t, 2), lax.rem(t, 2)].reshape(D, D)
+
+    for t in range(4):
+        cols = pl.ds(t * D, D)
+        tmp[...] = dot_nn(ml[...], wi[:, cols])
+        bias_t = row_of(bi, t * D)
+
+        def activate(i, carry):
+            rows = pl.ds(pl.multiple_of(i * 16, 16), 16)
+            u = tmp[rows, :] + bias_t
+            cdf = 0.5 * (1.0 + lax.erf(u * root_half))
+            act_s[rows, :] = (u * cdf).astype(BF16)
+            gp[rows, cols] = (cdf + u * inv_root_tau * jnp.exp(-0.5 * u * u)).astype(BF16)
+            return carry
+
+        lax.fori_loop(0, 30, activate, 0)
+        if t == 0:
+            n2[...] = dot_nn(act_s[...], wb_tile(t))
+        else:
+            n2[...] += dot_nn(act_s[...], wb_tile(t))
+        actT[cols, :] = act_s[...].T
+
+    gain2, shift2, bias2 = row_of(gf), row_of(sf), row_of(bb)
+
+    def norm_ffn_at(r0, size):
+        rows = pl.ds(r0, size)
+        hidden = n2[rows, :] + (n1[rows, :] * gain1 + shift1) + bias2
+        centered = hidden - jnp.mean(hidden, axis=-1, keepdims=True)
+        inv = lax.rsqrt(jnp.mean(centered * centered, axis=-1, keepdims=True) + ln_eps)
+        unit = centered * inv
+        n2[rows, :] = unit
+        r2[rows, :] = inv
+        return (unit * gain2 + shift2).astype(BF16)
+
+    qo_s[0:16, :] = norm_ffn_at(0, 16)
+    qo_s[16:32, :] = norm_ffn_at(16, 16)
+
+    def norm_ffn(i, carry):
+        po_s[pl.ds(pl.multiple_of(i * 16, 16), 16), :] = norm_ffn_at(pl.multiple_of(32 + i * 16, 16), 16)
+        return carry
+
+    lax.fori_loop(0, 27, norm_ffn, 0)
+    po_s[432:440, :] = norm_ffn_at(464, 16)[0:8]
+
+    slot_me = core * 16 + chip
+    base = pl.multiple_of(slot_me * 24, 8)
+    first_rows = (
+        qo_s[0:16, :].astype(F32)[0:1],
+        po_s[0:16, :].astype(F32)[0:1],
+        po_s[208:224, :].astype(F32)[12:13],
+    )
+    lane_row = iota((1, 128), 1)
+    meta = jnp.zeros((1, 128), F32)
+    for at, value in enumerate((
+        pvalid[0].astype(F32), pvalid[1].astype(F32), pos[0].astype(F32), neg[0].astype(F32), margin[0],
+    )):
+        meta = jnp.where(lane_row == at, value, meta)
+    pieces = [row[:, 128 * i:128 * i + 128] for row in first_rows for i in range(6)]
+    ex[pl.ds(base, 24), :] = jnp.concatenate(pieces + [meta, jnp.zeros((5, 128), F32)], axis=0)
+
+    pl.semaphore_wait(barrier, 16)
+    sends = []
+    for hop in range(1, 16):
+        block = ex.at[pl.ds(base, 24), :]
+        sends.append(pltpu.make_async_remote_copy(
+            src_ref=block, dst_ref=block, send_sem=ex_send.at[hop], recv_sem=ex_recv.at[hop],
+            device_id=(2 * lax.rem(chip + hop, 16) + core,), device_id_type=MESH,
+        ))
+        sends[-1].start()
+
+    out_q = pltpu.make_async_copy(qo_s, qout_h, out_sem.at[0])
+    out_p = pltpu.make_async_copy(po_s, pout_h, out_sem.at[1])
+    out_q.start()
+    out_p.start()
+
+    mlT[...] = ml[...].T
+    xT[...] = x_s[...].T
+    cT[...] = c_s[...].T
+    loads["qg"].wait()
+    loads["pg"].wait()
+
+    def ffn_norm_back(r0, upstream, sums):
+        rows = pl.ds(r0, 16)
+        unit = n2[rows, :]
+        scaled = upstream * gain2
+        hidden_grad = r2[rows, :] * (
+            scaled
+            - jnp.mean(scaled, axis=-1, keepdims=True)
+            - unit * jnp.mean(scaled * unit, axis=-1, keepdims=True)
+        )
+        n2[rows, :] = hidden_grad
+        rounded = hidden_grad.astype(BF16)
+        ml[rows, :] = rounded
+        return (
+            sums[0] + fold8(upstream * unit), sums[1] + fold8(upstream), sums[2] + fold8(rounded.astype(F32)),
+        )
+
+    def middle_block(i, sums):
+        upstream = pg_s[pl.ds(pl.multiple_of(i * 16, 16), 16), :].astype(F32)
+        return ffn_norm_back(pl.multiple_of(32 + i * 16, 16), upstream, sums)
+
+    zero8 = jnp.zeros((8, D), F32)
+    sums = (zero8, zero8, zero8)
+    sums = ffn_norm_back(16, qg_s[16:32, :].astype(F32), sums)
+    sums = lax.fori_loop(1, 13, middle_block, sums)
+    sums = lax.fori_loop(14, 27, middle_block, sums)
+    last = jnp.concatenate([pg_s[432:440, :].astype(F32), jnp.zeros((8, D), F32)], axis=0)
+    sums = ffn_norm_back(464, last, sums)
+
+    for send in sends:
+        send.wait()
+    same_core = ex.at[pl.ds(pl.multiple_of(core * 384, 8), 384), :]
+    across = pltpu.make_async_remote_copy(
+        src_ref=same_core, dst_ref=same_core, send_sem=ex_send.at[0], recv_sem=ex_recv.at[0],
+        device_id=(partner,), device_id_type=MESH,
+    )
+    across.start()
+    across.wait()
+
+    def first(r):
+        return ex[pl.ds(r, 32, stride=24), :]
+
+    cls_q = jnp.concatenate([first(i) for i in range(6)], axis=1)
+    cls_0 = jnp.concatenate([first(6 + i) for i in range(6)], axis=1).astype(BF16)
+    cls_1 = jnp.concatenate([first(12 + i) for i in range(6)], axis=1).astype(BF16)
+    metas = first(18)
+    metas_t = metas.T
+    s0 = score_scale * dot_nt(cls_q.astype(BF16), cls_0)
+    s1 = score_scale * dot_nt(cls_q.astype(BF16), cls_1)
+    col = iota((1, 32), 1)
+    passage = (4 * lax.rem(col, 16) + 2 * lax.div(col, 16)).astype(F32)
+    at_pos, at_neg, wanted = metas[:, 2:3], metas[:, 3:4], metas[:, 4:5]
+    pos0, pos1 = at_pos == passage, at_pos == passage + 1.0
+    neg0, neg1 = at_neg == passage, at_neg == passage + 1.0
+    m0 = jnp.where((metas_t[0:1, :] > 0.5) | pos0, s0, -1e30)
+    m1 = jnp.where((metas_t[1:2, :] > 0.5) | pos1, s1, -1e30)
+    peak = jnp.maximum(jnp.max(m0, axis=1, keepdims=True), jnp.max(m1, axis=1, keepdims=True))
+    total = jnp.sum(jnp.exp(m0 - peak), axis=1, keepdims=True) + jnp.sum(jnp.exp(m1 - peak), axis=1, keepdims=True)
+    lse = peak + jnp.log(total)
+
+    def picked(where0, where1):
+        return jnp.sum(jnp.where(where0, s0, 0.0), axis=1, keepdims=True) + jnp.sum(
+            jnp.where(where1, s1, 0.0), axis=1, keepdims=True
+        )
+
+    at_positive = picked(pos0, pos1)
+    miss = at_positive - picked(neg0, neg1) - wanted
+    losses = lse - at_positive + margin_weight * miss * miss
+    pos0, pos1, neg0, neg1 = (hit.astype(F32) for hit in (pos0, pos1, neg0, neg1))
+    ds0 = (jnp.exp(m0 - lse) - pos0 + 2.0 * margin_weight * miss * (pos0 - neg0)).astype(BF16)
+    ds1 = (jnp.exp(m1 - lse) - pos1 + 2.0 * margin_weight * miss * (pos1 - neg1)).astype(BF16)
+    mine = iota((32, 1), 0) == slot_me
+    mine_col = iota((1, 32), 1) == slot_me
+    loss_o[...] = jnp.sum(jnp.where(mine, losses, 0.0), axis=0, keepdims=True)
+    dq_all = score_scale * (dot_nn(ds0, cls_0) + dot_nn(ds1, cls_1))
+    d_query = jnp.sum(jnp.where(mine, dq_all, 0.0), axis=0, keepdims=True)
+
+    def passage_grad_row(ds):
+        column = jnp.sum(jnp.where(mine_col, ds.astype(F32), 0.0), axis=1, keepdims=True)
+        return score_scale * jnp.sum(column * cls_q, axis=0, keepdims=True)
+
+    d_first = (d_query, passage_grad_row(ds0), passage_grad_row(ds1))
+
+    row16 = iota((16, 1), 0)
+    for r0, at, source, add in (
+        (0, 0, qg_s[0:16, :], d_first[0]), (32, 0, pg_s[0:16, :], d_first[1]), (240, 12, pg_s[208:224, :], d_first[2]),
+    ):
+        upstream = source.astype(F32) + jnp.where(row16 == at, add, 0.0)
+        sums = ffn_norm_back(r0, upstream, sums)
+    vec[...] = jnp.zeros_like(vec)
+    vec[5:6, :] = jnp.sum(sums[2], axis=0, keepdims=True)
+    vec[6:7, :] = jnp.sum(sums[0], axis=0, keepdims=True)
+    vec[7:8, :] = jnp.sum(sums[1], axis=0, keepdims=True)
+
+    def chunk(k):
+        return g_s.at[k] if k < 4 else wb.at[k - 4]
+
+    def x_first(k):
+        return k % 2 == 0
+
+    def remote(source, target, send, recv, device):
+        return pltpu.make_async_remote_copy(
+            src_ref=source, dst_ref=target, send_sem=send, recv_sem=recv, device_id=(device,), device_id_type=MESH,
+        )
+
+    def step_c(k):
+        return remote(chunk(k).at[1 - core], rc.at[k % 2], c_send.at[k], c_recv.at[k], partner)
+
+    def step_a(k):
+        half_away = chunk(k).at[core, :, :, 1 - xx] if x_first(k) else chunk(k).at[core, :, 1 - yy]
+        return remote(half_away, ra.at[k], a_send.at[k], a_recv.at[k], x_peer if x_first(k) else y_peer)
+
+    def step_b(k):
+        away = chunk(k).at[core, :, 1 - yy, xx] if x_first(k) else chunk(k).at[core, :, yy, 1 - xx]
+        return remote(away, rb.at[k], b_send.at[k], b_recv.at[k], y_peer if x_first(k) else x_peer)
+
+    def step_z(k, hop):
+        to = lax.rem(zz + hop, 4)
+        return remote(
+            chunk(k).at[core, to, yy, xx], rz.at[k, hop - 1], z_send.at[k, hop - 1], z_recv.at[k, hop - 1],
+            to * 8 + plane,
+        )
+
+    def start_c(k):
+        if k >= 2:
+            pl.semaphore_wait(credit, 1)
+        step_c(k).start()
+
+    def end_c(k):
+        step_c(k).wait()
+
+        def add(z, carry):
+            for y in range(2):
+                for x in range(2):
+                    chunk(k)[core, z, y, x] += rc[k % 2, z, y, x]
+            return carry
+
+        lax.fori_loop(0, 4, add, 0)
+        if k < 4:
+            pl.semaphore_signal(credit, inc=1, device_id=(partner,), device_id_type=MESH)
+        step_a(k).start()
+
+    def end_a(k):
+        step_a(k).wait()
+
+        def add(z, carry):
+            for i in range(2):
+                if x_first(k):
+                    chunk(k)[core, z, i, xx] += ra[k, z, i]
+                else:
+                    chunk(k)[core, z, yy, i] += ra[k, z, i]
+            return carry
+
+        lax.fori_loop(0, 4, add, 0)
+        step_b(k).start()
+
+    def end_b(k):
+        step_b(k).wait()
+
+        def add(z, carry):
+            chunk(k)[core, z, yy, xx] += rb[k, z]
+            return carry
+
+        lax.fori_loop(0, 4, add, 0)
+        for hop in range(1, 4):
+            step_z(k, hop).start()
+
+    def end_z(k):
+        for hop in range(1, 4):
+            step_z(k, hop).wait()
+        total = chunk(k)[core, zz, yy, xx].astype(F32)
+        for hop in range(3):
+            total += rz[k, hop].astype(F32)
+        if k < 2:
+            wbg[48 * k:48 * k + 48, :] = total
+        elif k < 4:
+            at = (k - 2) * 1536
+            wig[:, at:at + 768] = total[0:24]
+            wig[:, at + 768:at + 1536] = total[24:48]
+        elif k == 4:
+            wvg[...] = total[0:24]
+            wog[...] = total[24:48]
+        else:
+            wqg[...] = total[0:24]
+            wkg[...] = total[24:48]
+
+    for h in range(2):
+        def back_grad(t, carry):
+            left = jnp.concatenate(
+                [actT[pl.ds(pl.multiple_of(t * D + 96 * i + 48 * h, 16), 48), :] for i in range(8)], axis=0
+            )
+            grad = dot_nn(left, ml[...]).astype(BF16)
+            for i in range(8):
+                chunk(h)[i % 2, t, i // 4, (i // 2) % 2] = grad[48 * i:48 * i + 48]
+            return carry
+
+        lax.fori_loop(0, 4, back_grad, 0)
+        start_c(h)
+
+    for t in range(4):
+        cols = pl.ds(t * D, D)
+        tmp[...] = dot_nt(ml[...], wb_tile(t))
+
+        def inner_back(i, total):
+            rows = pl.ds(pl.multiple_of(i * 16, 16), 16)
+            rounded = (tmp[rows, :] * gp[rows, cols].astype(F32)).astype(BF16)
+            gp[rows, cols] = rounded
+            return total + fold8(rounded.astype(F32))
+
+        total = lax.fori_loop(0, 30, inner_back, zero8)
+        vec[8 + t:9 + t, :] = jnp.sum(total, axis=0, keepdims=True)
+        n2[...] += dot_nt(gp[:, cols], wi[:, cols])
+        if t == 0:
+            end_c(0)
+        if t == 1:
+            end_c(1)
+
+    def pair_grad(k, left_0, right_0, left_1, right_1):
+        def group(t, carry):
+            rows = pl.ds(pl.multiple_of(t * 192, 16), 192)
+            grad_0 = dot_nn(left_0[rows, :], right_0[...]).reshape(8, 24, D)
+            grad_1 = dot_nn(left_1[rows, :], right_1[...]).reshape(8, 24, D)
+            both = jnp.concatenate([grad_0, grad_1], axis=1).astype(BF16)
+            for i in range(8):
+                chunk(k)[i % 2, t, i // 4, (i // 2) % 2] = both[i]
+            return carry
+
+        lax.fori_loop(0, 4, group, 0)
+        start_c(k)
+
+    for j in range(2):
+        pair_grad(2 + j, mlT, gp.at[:, pl.ds(2 * j * D, D)], mlT, gp.at[:, pl.ds((2 * j + 1) * D, D)])
+
+    def attn_norm_back(i, sums):
+        rows = pl.ds(pl.multiple_of(i * 16, 16), 16)
+        upstream, unit = n2[rows, :], n1[rows, :]
+        scaled = upstream * gain1
+        hidden_grad = r1[rows, :] * (
+            scaled
+            - jnp.mean(scaled, axis=-1, keepdims=True)
+            - unit * jnp.mean(scaled * unit, axis=-1, keepdims=True)
+        )
+        n1[rows, :] = hidden_grad
+        rounded = hidden_grad.astype(BF16)
+        ml[rows, :] = rounded
+        return (
+            sums[0] + fold8(upstream * unit), sums[1] + fold8(upstream), sums[2] + fold8(rounded.astype(F32)),
+        )
+
+    sums = lax.fori_loop(0, 30, attn_norm_back, (zero8, zero8, zero8))
+    vec[2:3, :] = jnp.sum(sums[2], axis=0, keepdims=True)
+    vec[3:4, :] = jnp.sum(sums[0], axis=0, keepdims=True)
+    vec[4:5, :] = jnp.sum(sums[1], axis=0, keepdims=True)
+    c_s[...] = dot_nt(ml[...], wo[...]).astype(BF16)
+    end_c(2)
+    end_c(3)
+
+    q_rows, k_rows, v_rows = spread(q_s[0:32, :]), k_s[0:32, :], v_s[0:32, :]
+    dc_rows = spread(c_s[0:32, :])
+    soft = pq_s[...]
+    dp = dot_nt(v_rows, dc_rows)
+    soft_f = soft.astype(F32)
+    ds = (soft_f * (dp - jnp.sum(soft_f * dp, axis=0, keepdims=True))).astype(BF16)
+    v_s[0:32, :] = dot_nn(soft, dc_rows).astype(BF16)
+    k_s[0:32, :] = dot_nn(ds, q_rows).astype(BF16)
+    q_s[0:32, :] = (0.125 * gather_heads(dot_tn(ds, k_rows))).astype(BF16)
+
+    def attend_back(pair, carry):
+        lanes = pl.ds(pl.multiple_of(pair * 128, 128), 128)
+        for slot in range(2):
+            low_at = 12 * slot
+            rows = pl.ds(32 + 208 * slot, WIN)
+            keys, queries, values = k_s[rows, lanes], q_s[rows, lanes], v_s[rows, lanes]
+            inside = ((key_at >= low_at) & (key_at < low_at + SLOT)).astype(BF16)
+            upstream = c_s[rows, lanes] * inside
+            keys_t = keys.T
+            parts, dv, dk = [], 0.0, 0.0
+            for h in range(2):
+                p = p_s[slot, 2 * pair + h]
+                dc = upstream * half[h]
+                dp = dot_nt(values, dc)
+                pf = p.astype(F32)
+                ds = (pf * (dp - jnp.sum(pf * dp, axis=0, keepdims=True))).astype(BF16)
+                dv += dot_nn(p, dc)
+                dk += dot_nn(ds, queries * half[h])
+                parts.append(dot_nn(keys_t, ds)[64 * h:64 * h + 64, :])
+            dq = 0.125 * jnp.concatenate(parts, axis=0).T
+            for ref, new in ((q_s, dq), (k_s, dk), (v_s, dv)):
+                if slot == 0:
+                    ref[32:240, lanes] = new[0:208].astype(BF16)
+                    old = ref[240:272, lanes].astype(F32)
+                    ref[240:272, lanes] = jnp.where(iota((32, 128), 0) < 12, new[208:240], old).astype(BF16)
+                else:
+                    old = ref[240:256, lanes].astype(F32)
+                    ref[240:256, lanes] = jnp.where(iota((16, 128), 0) >= 12, new[0:16], old).astype(BF16)
+                    ref[256:480, lanes] = new[16:240].astype(BF16)
+        return carry
+
+    lax.fori_loop(0, 3, attend_back, 0)
+    end_a(0)
+    end_a(1)
+    lax.fori_loop(3, 6, attend_back, 0)
+
+    def column_sum(ref):
+        def step(i, total):
+            return total + fold8(ref[pl.ds(pl.multiple_of(i * 16, 16), 16), :].astype(F32))
+
+        return jnp.sum(lax.fori_loop(0, 30, step, zero8), axis=0, keepdims=True)
+
+    vec[0:1, :] = column_sum(q_s)
+    vec[1:2, :] = column_sum(v_s)
+    end_b(0)
+    end_b(1)
+    pair_grad(4, xT, v_s, cT, ml)
+    pair_grad(5, xT, q_s, xT, k_s)
+
+    def vec_step(i, device):
+        return remote(vec, vecr.at[i], v_send.at[i], v_recv.at[i], device)
+
+    vec_step(0, partner).start()
+    end_c(4)
+    end_c(5)
+    n1[...] += dot_nt(q_s[...], wq[...])
+    vec_step(0, partner).wait()
+    vec[...] += vecr[0]
+    vec_step(1, x_peer).start()
+    n1[...] += dot_nt(k_s[...], wk[...])
+    vec_step(1, x_peer).wait()
+    vec[...] += vecr[1]
+    vec_step(2, y_peer).start()
+    n1[...] += dot_nt(v_s[...], wv[...])
+    vec_step(2, y_peer).wait()
+    vec[...] += vecr[2]
+
+    def vec_z(hop):
+        return remote(
+            vec, vecz.at[hop - 1], v_send.at[2 + hop], v_recv.at[2 + hop], lax.rem(zz + hop, 4) * 8 + plane
+        )
+
+    for hop in range(1, 4):
+        vec_z(hop).start()
+    out_qg = pltpu.make_async_copy(n1.at[0:32, :], qtg_h, out_sem.at[2])
+    out_pg = pltpu.make_async_copy(n1.at[32:472, :], ptg_h, out_sem.at[3])
+    out_qg.start()
+    out_pg.start()
+    end_z(0)
+    end_z(1)
+    for hop in range(1, 4):
+        vec_z(hop).wait()
+    whole = vec[...] + vecz[0] + vecz[1] + vecz[2]
+    small = pltpu.roll(whole, D - 24 * me, 1)
+    for at, ref in enumerate((bqg, bvg, bog, gag, sag, bbg, gfg, sfg)):
+        ref[...] = small[at:at + 1, 0:24]
+    wide = pltpu.roll(whole[8:16], D - 96 * plane, 1)
+    big[...] = jnp.sum(jnp.where(iota((8, D), 0) == zz, wide, 0.0), axis=0, keepdims=True)[:, 0:96]
+
+    end_a(2)
+    end_a(3)
+    end_b(2)
+    end_b(3)
+    end_a(4)
+    end_a(5)
+    end_z(2)
+    end_z(3)
+    end_b(4)
+    end_b(5)
+    end_z(4)
+    end_z(5)
+    out_q.wait()
+    out_p.wait()
+    out_qg.wait()
+    out_pg.wait()
+
+
+def on_device_small(*operands):
+    (
+        query_tokens, passage_tokens, query_lengths, passage_lengths, passage_valid, positives, negatives,
+        teacher_margins, query_grad, passage_grad, weight_query, bias_query, weight_key, weight_value, bias_value,
+        weight_out, bias_out, gain_attn, shift_attn, weight_in, bias_in, weight_back, bias_back, gain_ffn, shift_ffn,
+    ) = operands
+    hbm, vmem, smem = (pl.BlockSpec(memory_space=space) for space in (pl.ANY, pltpu.VMEM, pltpu.SMEM))
+    shape = jax.ShapeDtypeStruct
+    slabs = (2, 2, 4, 2, 2, 48, D)
+    outs = pl.pallas_call(
+        layer_kernel,
+        out_shape=(
+            shape((32, D), BF16), shape((440, D), BF16), shape((1, 1), F32), shape((32, D), F32), shape((440, D), F32),
+            shape((24, D), F32), shape((1, 24), F32), shape((24, D), F32), shape((24, D), F32), shape((1, 24), F32),
+            shape((24, D), F32), shape((1, 24), F32), shape((1, 24), F32), shape((1, 24), F32),
+            shape((24, FF), F32), shape((1, 96), F32), shape((96, D), F32), shape((1, 24), F32), shape((1, 24), F32),
+            shape((1, 24), F32),
+        ),
+        in_specs=[
+            hbm, hbm, smem, smem, smem, smem, smem, smem, hbm, hbm,
+            hbm, vmem, hbm, hbm, vmem, hbm, vmem, vmem, vmem, hbm, vmem, hbm, vmem, vmem, vmem,
+        ],
+        out_specs=(hbm, hbm, vmem, hbm, hbm) + (vmem,) * 15,
+        scratch_shapes=[
+            pltpu.VMEM((D, D), BF16), pltpu.VMEM((D, D), BF16), pltpu.VMEM((D, D), BF16), pltpu.VMEM((D, D), BF16),
+            pltpu.VMEM((D, FF), BF16), pltpu.VMEM(slabs, BF16),
+            pltpu.VMEM((440, D), BF16), pltpu.VMEM((ROWS, D), BF16), pltpu.VMEM((D, ROWS), BF16),
+            pltpu.VMEM((ROWS, D), BF16), pltpu.VMEM((ROWS, D), BF16), pltpu.VMEM((ROWS, D), BF16),
+            pltpu.VMEM((2, 12, WIN, WIN), BF16), pltpu.VMEM((32, 384), BF16),
+            pltpu.VMEM((ROWS, D), BF16), pltpu.VMEM((D, ROWS), BF16),
+            pltpu.VMEM((ROWS, D), F32), pltpu.VMEM((ROWS, D), F32), pltpu.VMEM((ROWS, 1), F32), pltpu.VMEM((ROWS, 1), F32),
+            pltpu.VMEM((ROWS, D), BF16), pltpu.VMEM((D, ROWS), BF16),
+            pltpu.VMEM((ROWS, D), BF16), pltpu.VMEM((FF, ROWS), BF16), pltpu.VMEM((ROWS, D), F32),
+            pltpu.VMEM((ROWS, FF), BF16),
+            pltpu.VMEM((32, D), BF16), pltpu.VMEM((440, D), BF16), pltpu.VMEM((32, D), BF16), pltpu.VMEM((440, D), BF16),
+            pltpu.VMEM((768, 128), F32), pltpu.VMEM((8, D), F32),
+            pltpu.VMEM((16, D), F32), pltpu.VMEM((3, 16, D), F32), pltpu.VMEM((3, 16, D), F32),
+            pltpu.VMEM((4, 2, 4, 2, 2, 48, D), BF16),
+            pltpu.VMEM((2, 4, 2, 2, 48, D), BF16), pltpu.VMEM((6, 4, 2, 48, D), BF16), pltpu.VMEM((6, 4, 48, D), BF16),
+            pltpu.VMEM((6, 3, 48, D), BF16),
+            pltpu.SemaphoreType.DMA((10,)), pltpu.SemaphoreType.DMA((4,)),
+            pltpu.SemaphoreType.DMA((16,)), pltpu.SemaphoreType.DMA((16,)),
+            pltpu.SemaphoreType.DMA((6,)), pltpu.SemaphoreType.DMA((6,)),
+            pltpu.SemaphoreType.DMA((6,)), pltpu.SemaphoreType.DMA((6,)),
+            pltpu.SemaphoreType.DMA((6,)), pltpu.SemaphoreType.DMA((6,)),
+            pltpu.SemaphoreType.DMA((6, 3)), pltpu.SemaphoreType.DMA((6, 3)),
+            pltpu.SemaphoreType.DMA((6,)), pltpu.SemaphoreType.DMA((6,)),
+            pltpu.SemaphoreType.REGULAR,
+        ],
+        compiler_params=pltpu.CompilerParams(
+            collective_id=0, has_side_effects=True, vmem_limit_bytes=64 * 1024 * 1024 - 65536,
+        ),
+        name="encoder_layer",
+    )(
+        query_tokens, passage_tokens, query_lengths, passage_lengths, passage_valid, positives, negatives,
+        teacher_margins, query_grad, passage_grad, weight_query, bias_query, weight_key, weight_value, bias_value,
+        weight_out, bias_out, gain_attn, shift_attn, weight_in, bias_in, weight_back.reshape(slabs), bias_back,
+        gain_ffn, shift_ffn,
+    )
+    flat = lambda array: array.reshape(-1)
+    return tuple(flat(out) if out.shape[0] == 1 else out for out in outs)
+
+
 def solution(mesh):
     return jax.shard_map(
-        on_device,
+        on_device_small if mesh.shape["dp"] == 32 else on_device,
         mesh=mesh,
         in_specs=(
             P("dp", None),

time: 1040 us -> 170 us (0.16)
  waiting for transfers between devices: 679 us -> 0 us
  Pallas kernels: 0 us -> 150 us
  blocking collectives: 125 us -> 0 us
  matrix products: 110 us -> 0 us
  local copies, waits for them, and re-layouts: 74.9 us -> 13.9 us
  other arithmetic: 21.4 us -> 0 us
  between operations: 23.1 us -> 5.07 us
    reduce_scatter x3 -> x0, waiting for transfers between devices: 388 us -> none  [the longest x1 142 us: on_device(): lax.psum_scatter(back_weight_grad, 'dp', scatter_dimension=0, tiled=True)]
    unnamed x11 -> x0, waiting for transfers between devices: 291 us -> none
    pallas_call x0 -> x1, Pallas kernels: none -> 150 us  [on_device_small(): pl.pallas_call(layer_kernel, out_shape=(shape((32, D), BF16), shape((440,...]
    dot_general x50 -> x0, matrix products: 110 us -> none  [the longest x12 36.8 us: left_across(): lax.dot_general(left, right, (((0,), (0,)), ((), ())), preferred_element_...]
    unnamed x2 -> x0, blocking collectives: 84.2 us -> none
    all_gather x1 -> x0, blocking collectives: 40.7 us -> none  [on_device(): lax.all_gather(cls_passage, 'dp', axis=0, tiled=True)]
    reshape x11 -> x0, local copies, waits for them, and re-layouts: 25.7 us -> none  [the longest x2 4.87 us: on_device(): passage_upstream = passage_grad.astype(jnp.float32).reshape(passage_slots...]
    convert_element_type x16 -> x0, local copies, waits for them, and re-layouts: 18.5 us -> none  [the longest x4 5.11 us: encode_forward(): context = context.reshape(row_count, D).astype(jnp.bfloat16)]
  transfers between devices with their start and end apart: 7 -> 0, of which waited for: 6 -> 0; matrix products, arithmetic and copies ran while one was open for 8% -> 0% of each run, Pallas kernels for 0% -> 0%
where the time goes in v1:
time: 170 us; the launch traced here: 169 us
  Pallas kernels  150 us (88%)
  local copies, waits for them, and re-layouts  13.9 us (8%)
  between operations  5.07 us (3%)
    pallas_call x1, Pallas kernels, on_device_small(): pl.pallas_call(layer_kernel, out_shape=(shape((32, D), BF16), shape((440,...  150 us
    unnamed x53, local copies, waits for them, and re-layouts  13.9 us

profile of v1, /device:TPU:0, one launch (start us, length us, event | category | flops | bytes accessed | tf_op | source)
XLA Modules:
  0.0 169.3 jit_solution(3490459840796871462)
XLA Ops:
  3.2 150.3 %encoder_layer.1 = (bf16[32,768]{1,0:T(8,128)(2,1)}, bf16[440,768]{1,0:T(8,128)(2,1)}, f32[1,1]{1,0:T(1,128)}, f32[32,768]{1,0:T(8,128)}, f32[440,768]{1,0:T(8,1...) custom-call(bf16[32,768]{1,0:T(8,128)(2,1)} %qtok.1, ...), custom_call_target="tpu_custom_call" | custom-call | tf_op jit(solution)/shard_map/encoder_layer/pallas_call | solution.py:1056
  153.6 0.0 copy-start.3
  153.6 0.0 copy-start
  153.6 1.5 copy.69
  155.1 2.0 %copy.70 = bf16[440,768]{1,0:T(8,128)(2,1)} copy(bf16[440,768]{1,0:T(8,128)(2,1)} %get-tuple-element.81) | data formatting | bytes 1351680
  157.7 0.0 copy-done.3
  157.7 0.6 copy.72
  158.3 0.0 copy-done
  158.3 0.0 copy-start.5
  158.4 0.0 copy-start.15
  158.4 0.0 copy-start.4
  158.4 0.0 copy-start.14
  158.4 0.0 copy-start.13
  158.4 0.0 copy-start.12
  158.4 0.0 copy-start.2
  158.4 0.0 copy-start.11
  158.4 0.0 copy-start.1
  158.4 1.1 copy.73
  159.5 0.0 copy-done.7
  159.5 0.6 copy.74
  160.2 0.0 copy-done.16
  160.2 0.5 copy.75
  160.7 0.0 copy-done.6
  160.7 0.6 copy.76
  161.3 0.0 copy-done.5
  161.3 0.6 copy.77
  161.9 0.0 copy-done.15
  161.9 0.5 copy.78
  162.5 0.0 copy-done.4
  162.5 0.6 copy.79
  163.1 0.0 copy-done.14
  163.1 0.5 copy.80
  163.6 0.0 copy-done.13
  163.6 0.5 copy.81
  164.1 0.0 copy-done.12
  164.1 0.5 copy.82
  164.6 0.0 copy-done.2
  164.6 0.7 copy.83
  165.4 0.0 copy-done.11
  165.4 0.5 copy.84
  165.9 0.0 copy-done.1
  165.9 0.7 copy.85
  166.6 0.0 copy-done.10
  166.6 0.5 copy.86
  167.1 0.0 copy-done.9
  167.1 0.5 copy.87
  167.6 0.0 copy-done.8
  167.6 0.5 copy.88
  (6 shorter events, 0.0 us)
Async XLA Ops:
  153.6 4.1 %copy-start.3 = (f32[32,768]{1,0:T(8,128)S(1)}, f32[32,768]{1,0:T(8,128)}, u32[]{:S(2)}) copy-start(f32[32,768]{1,0:T(8,128)} %get-tuple-element.83) | copy-start | bytes 294916
  153.6 4.7 %copy-start = (f32[440,768]{1,0:T(8,128)S(1)}, f32[440,768]{1,0:T(8,128)}, u32[]{:S(2)}) copy-start(f32[440,768]{1,0:T(8,128)} %get-tuple-element.84) | copy-start | bytes 4055044
  158.3 1.2 copy-start.7
  158.3 1.8 %copy-start.16 = (f32[1,24]{1,0:T(1,128)S(1)}, f32[1,24]{1,0:T(1,128)}, u32[]{:S(2)}) copy-start(f32[1,24]{1,0:T(1,128)} %get-tuple-element.46) | copy-start | bytes 292
  158.3 2.3 %copy-start.6 = (f32[24,768]{1,0:T(8,128)S(1)}, f32[24,768]{1,0:T(8,128)}, u32[]{:S(2)}) copy-start(f32[24,768]{1,0:T(8,128)} %get-tuple-element.87) | copy-start | bytes 221188
  158.3 3.0 %copy-start.5 = (f32[24,768]{1,0:T(8,128)S(1)}, f32[24,768]{1,0:T(8,128)}, u32[]{:S(2)}) copy-start(f32[24,768]{1,0:T(8,128)} %get-tuple-element.88) | copy-start | bytes 221188
  158.4 3.6 %copy-start.15 = (f32[1,24]{1,0:T(1,128)S(1)}, f32[1,24]{1,0:T(1,128)}, u32[]{:S(2)}) copy-start(f32[1,24]{1,0:T(1,128)} %get-tuple-element.49) | copy-start | bytes 292
  158.4 4.1 %copy-start.4 = (f32[24,768]{1,0:T(8,128)S(1)}, f32[24,768]{1,0:T(8,128)}, u32[]{:S(2)}) copy-start(f32[24,768]{1,0:T(8,128)} %get-tuple-element.90) | copy-start | bytes 221188
  158.4 4.7 %copy-start.14 = (f32[1,24]{1,0:T(1,128)S(1)}, f32[1,24]{1,0:T(1,128)}, u32[]{:S(2)}) copy-start(f32[1,24]{1,0:T(1,128)} %get-tuple-element.51) | copy-start | bytes 292
  158.4 5.2 %copy-start.13 = (f32[1,24]{1,0:T(1,128)S(1)}, f32[1,24]{1,0:T(1,128)}, u32[]{:S(2)}) copy-start(f32[1,24]{1,0:T(1,128)} %get-tuple-element.52) | copy-start | bytes 292
  158.4 5.7 %copy-start.12 = (f32[1,24]{1,0:T(1,128)S(1)}, f32[1,24]{1,0:T(1,128)}, u32[]{:S(2)}) copy-start(f32[1,24]{1,0:T(1,128)} %get-tuple-element.53) | copy-start | bytes 292
  158.4 6.2 %copy-start.2 = (f32[24,3072]{1,0:T(8,128)S(1)}, f32[24,3072]{1,0:T(8,128)}, u32[]{:S(2)}) copy-start(f32[24,3072]{1,0:T(8,128)} %get-tuple-element.94) | copy-start | bytes 884740
  158.4 6.9 %copy-start.11 = (f32[1,96]{1,0:T(1,128)S(1)}, f32[1,96]{1,0:T(1,128)}, u32[]{:S(2)}) copy-start(f32[1,96]{1,0:T(1,128)} %get-tuple-element.55) | copy-start | bytes 1156
  158.4 7.4 %copy-start.1 = (f32[96,768]{1,0:T(8,128)S(1)}, f32[96,768]{1,0:T(8,128)}, u32[]{:S(2)}) copy-start(f32[96,768]{1,0:T(8,128)} %get-tuple-element.96) | copy-start | bytes 884740
  159.5 7.1 %copy-start.10 = (f32[1,24]{1,0:T(1,128)S(1)}, f32[1,24]{1,0:T(1,128)}, u32[]{:S(2)}) copy-start(f32[1,24]{1,0:T(1,128)} %get-tuple-element.57) | copy-start | bytes 292
  159.5 7.6 %copy-start.9 = (f32[1,24]{1,0:T(1,128)S(1)}, f32[1,24]{1,0:T(1,128)}, u32[]{:S(2)}) copy-start(f32[1,24]{1,0:T(1,128)} %get-tuple-element.58) | copy-start | bytes 292
  159.5 8.1 %copy-start.8 = (f32[1,24]{1,0:T(1,128)S(1)}, f32[1,24]{1,0:T(1,128)}, u32[]{:S(2)}) copy-start(f32[1,24]{1,0:T(1,128)} %get-tuple-element.59) | copy-start | bytes 292

commit v2 on v1

--- a/solution.py
+++ b/solution.py
@@ -470,8 +470,7 @@
 def layer_kernel(
     qtok, ptok, qlen, plen, pvalid, pos, neg, margin, qgrad, pgrad,
     wq_h, bq, wk_h, wv_h, bv, wo_h, bo, ga, sa, wi_h, bi, wb_h, bb, gf, sf,
-    qout_h, pout_h, loss_o, qtg_h, ptg_h, wqg, bqg, wkg, wvg, bvg, wog, bog, gag, sag,
-    wig, big, wbg, bbg, gfg, sfg,
+    qout_h, pout_h, qtg_h, ptg_h, wqg, wkg, wvg, wog, wig, wbg, small_o,
     wq, wk, wv, wo, wi, wb, pstage, x_s, xT, q_s, k_s, v_s, p_s, pq_s, c_s, cT, n1, n2, r1, r2,
     ml, mlT, act_s, actT, tmp, gp, qg_s, pg_s, qo_s, po_s, ex, dcls, vec, vecr, vecz,
     g_s, rc, ra, rb, rz,
@@ -490,12 +489,16 @@
     plane = lax.rem(me, 8)
 
     loads = {}
-    for at, (name, source, target) in enumerate((
-        ("ptok", ptok, pstage), ("qtok", qtok, qo_s), ("wq", wq_h, wq), ("wk", wk_h, wk), ("wv", wv_h, wv),
-        ("wo", wo_h, wo), ("wi", wi_h, wi), ("wb", wb_h, wb), ("qg", qgrad, qg_s), ("pg", pgrad, pg_s),
-    )):
-        loads[name] = pltpu.make_async_copy(source, target, load_sem.at[at])
+
+    def load(name, source, target):
+        loads[name] = pltpu.make_async_copy(source, target, load_sem.at[len(loads)])
         loads[name].start()
+
+    load("ptok", ptok, pstage)
+    load("qtok", qtok, qo_s)
+    load("wq", wq_h, wq)
+    load("wk", wk_h, wk)
+    load("wv", wv_h, wv)
 
     barrier = pltpu.get_barrier_semaphore()
     for hop in range(1, 16):
@@ -517,10 +520,16 @@
     ).astype(BF16)
 
     loads["wq"].wait()
+    load("wo", wo_h, wo)
+    load("wi", wi_h, wi)
     q_s[...] = ((dot_nn(x_s[...], wq[...]) + row_of(bq)).astype(BF16) * 0.125).astype(BF16)
     loads["wk"].wait()
     k_s[...] = dot_nn(x_s[...], wk[...]).astype(BF16)
     loads["wv"].wait()
+    for h in range(2):
+        load("wb" + str(h), wb_h.at[:, :, :, :, :, :, pl.ds(384 * h, 384)], wb.at[h])
+    load("qg", qgrad, qg_s)
+    load("pg", pgrad, pg_s)
     v_s[...] = (dot_nn(x_s[...], wv[...]) + row_of(bv)).astype(BF16)
 
     head_of = iota((12, 1, D), 2) // 64
@@ -574,7 +583,7 @@
     gain1, shift1, bias1 = row_of(ga), row_of(sa), row_of(bo)
 
     def norm_attn(i, carry):
-        rows = pl.ds(pl.multiple_of(i * 16, 16), 16)
+        rows = pl.ds(pl.multiple_of(i * 48, 16), 48)
         hidden = tmp[rows, :] + x_s[rows, :].astype(F32) + bias1
         centered = hidden - jnp.mean(hidden, axis=-1, keepdims=True)
         inv = lax.rsqrt(jnp.mean(centered * centered, axis=-1, keepdims=True) + ln_eps)
@@ -584,13 +593,14 @@
         ml[rows, :] = (unit * gain1 + shift1).astype(BF16)
         return carry
 
-    lax.fori_loop(0, 30, norm_attn, 0)
+    lax.fori_loop(0, 10, norm_attn, 0)
 
     loads["wi"].wait()
-    loads["wb"].wait()
+    loads["wb0"].wait()
+    loads["wb1"].wait()
 
     def wb_tile(t):
-        return wb[lax.div(t, 2), lax.rem(t, 2)].reshape(D, D)
+        return jnp.concatenate([wb[h, t // 2, t % 2].reshape(D, 384) for h in range(2)], axis=1)
 
     for t in range(4):
         cols = pl.ds(t * D, D)
@@ -624,14 +634,13 @@
         r2[rows, :] = inv
         return (unit * gain2 + shift2).astype(BF16)
 
-    qo_s[0:16, :] = norm_ffn_at(0, 16)
-    qo_s[16:32, :] = norm_ffn_at(16, 16)
+    qo_s[...] = norm_ffn_at(0, 32)
 
     def norm_ffn(i, carry):
-        po_s[pl.ds(pl.multiple_of(i * 16, 16), 16), :] = norm_ffn_at(pl.multiple_of(32 + i * 16, 16), 16)
+        po_s[pl.ds(pl.multiple_of(i * 48, 16), 48), :] = norm_ffn_at(pl.multiple_of(32 + i * 48, 16), 48)
         return carry
 
-    lax.fori_loop(0, 27, norm_ffn, 0)
+    lax.fori_loop(0, 9, norm_ffn, 0)
     po_s[432:440, :] = norm_ffn_at(464, 16)[0:8]
 
     slot_me = core * 16 + chip
@@ -672,7 +681,7 @@
     loads["pg"].wait()
 
     def ffn_norm_back(r0, upstream, sums):
-        rows = pl.ds(r0, 16)
+        rows = pl.ds(r0, upstream.shape[0])
         unit = n2[rows, :]
         scaled = upstream * gain2
         hidden_grad = r2[rows, :] * (
@@ -688,16 +697,15 @@
         )
 
     def middle_block(i, sums):
-        upstream = pg_s[pl.ds(pl.multiple_of(i * 16, 16), 16), :].astype(F32)
-        return ffn_norm_back(pl.multiple_of(32 + i * 16, 16), upstream, sums)
+        upstream = pg_s[pl.ds(pl.multiple_of(i * 32, 16), 32), :].astype(F32)
+        return ffn_norm_back(pl.multiple_of(32 + i * 32, 16), upstream, sums)
 
     zero8 = jnp.zeros((8, D), F32)
     sums = (zero8, zero8, zero8)
-    sums = ffn_norm_back(16, qg_s[16:32, :].astype(F32), sums)
-    sums = lax.fori_loop(1, 13, middle_block, sums)
-    sums = lax.fori_loop(14, 27, middle_block, sums)
-    last = jnp.concatenate([pg_s[432:440, :].astype(F32), jnp.zeros((8, D), F32)], axis=0)
-    sums = ffn_norm_back(464, last, sums)
+    sums = lax.fori_loop(1, 6, middle_block, sums)
+    sums = lax.fori_loop(7, 13, middle_block, sums)
+    last = jnp.concatenate([pg_s[416:440, :].astype(F32), jnp.zeros((8, D), F32)], axis=0)
+    sums = ffn_norm_back(448, last, sums)
 
     for send in sends:
         send.wait()
@@ -743,7 +751,7 @@
     ds1 = (jnp.exp(m1 - lse) - pos1 + 2.0 * margin_weight * miss * (pos1 - neg1)).astype(BF16)
     mine = iota((32, 1), 0) == slot_me
     mine_col = iota((1, 32), 1) == slot_me
-    loss_o[...] = jnp.sum(jnp.where(mine, losses, 0.0), axis=0, keepdims=True)
+    small_o[9:10, :] = jnp.sum(jnp.where(mine, losses, 0.0), axis=0, keepdims=True) + jnp.zeros((1, 128), F32)
     dq_all = score_scale * (dot_nn(ds0, cls_0) + dot_nn(ds1, cls_1))
     d_query = jnp.sum(jnp.where(mine, dq_all, 0.0), axis=0, keepdims=True)
 
@@ -753,108 +761,114 @@
 
     d_first = (d_query, passage_grad_row(ds0), passage_grad_row(ds1))
 
-    row16 = iota((16, 1), 0)
+    row32 = iota((32, 1), 0)
     for r0, at, source, add in (
-        (0, 0, qg_s[0:16, :], d_first[0]), (32, 0, pg_s[0:16, :], d_first[1]), (240, 12, pg_s[208:224, :], d_first[2]),
+        (0, 0, qg_s[...], d_first[0]), (32, 0, pg_s[0:32, :], d_first[1]), (224, 28, pg_s[192:224, :], d_first[2]),
     ):
-        upstream = source.astype(F32) + jnp.where(row16 == at, add, 0.0)
+        upstream = source.astype(F32) + jnp.where(row32 == at, add, 0.0)
         sums = ffn_norm_back(r0, upstream, sums)
     vec[...] = jnp.zeros_like(vec)
     vec[5:6, :] = jnp.sum(sums[2], axis=0, keepdims=True)
     vec[6:7, :] = jnp.sum(sums[0], axis=0, keepdims=True)
     vec[7:8, :] = jnp.sum(sums[1], axis=0, keepdims=True)
 
-    def chunk(k):
-        return g_s.at[k] if k < 4 else wb.at[k - 4]
-
-    def x_first(k):
-        return k % 2 == 0
+    def chunk(p, h):
+        return g_s.at[p, h] if p < 4 else wb.at[h, p - 4]
 
     def remote(source, target, send, recv, device):
         return pltpu.make_async_remote_copy(
             src_ref=source, dst_ref=target, send_sem=send, recv_sem=recv, device_id=(device,), device_id_type=MESH,
         )
 
-    def step_c(k):
-        return remote(chunk(k).at[1 - core], rc.at[k % 2], c_send.at[k], c_recv.at[k], partner)
-
-    def step_a(k):
-        half_away = chunk(k).at[core, :, :, 1 - xx] if x_first(k) else chunk(k).at[core, :, 1 - yy]
-        return remote(half_away, ra.at[k], a_send.at[k], a_recv.at[k], x_peer if x_first(k) else y_peer)
-
-    def step_b(k):
-        away = chunk(k).at[core, :, 1 - yy, xx] if x_first(k) else chunk(k).at[core, :, yy, 1 - xx]
-        return remote(away, rb.at[k], b_send.at[k], b_recv.at[k], y_peer if x_first(k) else x_peer)
-
-    def step_z(k, hop):
+    def step_c(p, h):
+        return remote(chunk(p, h).at[1 - core], rc.at[p % 2, h], c_send.at[p, h], c_recv.at[p, h], partner)
+
+    def step_a(p, h):
+        away = chunk(p, h).at[core, :, 1 - yy] if h else chunk(p, h).at[core, :, :, 1 - xx]
+        return remote(away, ra.at[p, h], a_send.at[p, h], a_recv.at[p, h], y_peer if h else x_peer)
+
+    def step_b(p, h):
+        away = chunk(p, h).at[core, :, yy, 1 - xx] if h else chunk(p, h).at[core, :, 1 - yy, xx]
+        return remote(away, rb.at[p, h], b_send.at[p, h], b_recv.at[p, h], x_peer if h else y_peer)
+
+    def step_z(p, h, hop):
         to = lax.rem(zz + hop, 4)
         return remote(
-            chunk(k).at[core, to, yy, xx], rz.at[k, hop - 1], z_send.at[k, hop - 1], z_recv.at[k, hop - 1],
+            chunk(p, h).at[core, to, yy, xx], rz.at[p, h, hop - 1], z_send.at[p, h, hop - 1], z_recv.at[p, h, hop - 1],
             to * 8 + plane,
         )
 
-    def start_c(k):
-        if k >= 2:
-            pl.semaphore_wait(credit, 1)
-        step_c(k).start()
-
-    def end_c(k):
-        step_c(k).wait()
-
-        def add(z, carry):
-            for y in range(2):
-                for x in range(2):
-                    chunk(k)[core, z, y, x] += rc[k % 2, z, y, x]
-            return carry
-
-        lax.fori_loop(0, 4, add, 0)
-        if k < 4:
-            pl.semaphore_signal(credit, inc=1, device_id=(partner,), device_id_type=MESH)
-        step_a(k).start()
-
-    def end_a(k):
-        step_a(k).wait()
-
-        def add(z, carry):
-            for i in range(2):
-                if x_first(k):
-                    chunk(k)[core, z, i, xx] += ra[k, z, i]
-                else:
-                    chunk(k)[core, z, yy, i] += ra[k, z, i]
-            return carry
-
-        lax.fori_loop(0, 4, add, 0)
-        step_b(k).start()
-
-    def end_b(k):
-        step_b(k).wait()
-
-        def add(z, carry):
-            chunk(k)[core, z, yy, xx] += rb[k, z]
-            return carry
-
-        lax.fori_loop(0, 4, add, 0)
-        for hop in range(1, 4):
-            step_z(k, hop).start()
-
-    def end_z(k):
-        for hop in range(1, 4):
-            step_z(k, hop).wait()
-        total = chunk(k)[core, zz, yy, xx].astype(F32)
-        for hop in range(3):
-            total += rz[k, hop].astype(F32)
-        if k < 2:
-            wbg[48 * k:48 * k + 48, :] = total
-        elif k < 4:
-            at = (k - 2) * 1536
-            wig[:, at:at + 768] = total[0:24]
-            wig[:, at + 768:at + 1536] = total[24:48]
-        elif k == 4:
-            wvg[...] = total[0:24]
-            wog[...] = total[24:48]
-        else:
-            wqg[...] = total[0:24]
-            wkg[...] = total[24:48]
+    def start_c(p):
+        for h in range(2):
+            if p >= 2:
+                pl.semaphore_wait(credit, 1)
+            step_c(p, h).start()
+
+    def end_c(p):
+        for h in range(2):
+            step_c(p, h).wait()
+
+            def add(z, carry):
+                for y in range(2):
+                    for x in range(2):
+                        chunk(p, h)[core, z, y, x] += rc[p % 2, h, z, y, x]
+                return carry
+
+            lax.fori_loop(0, 4, add, 0)
+            step_a(p, h).start()
+            if p < 4:
+                pl.semaphore_signal(credit, inc=1, device_id=(partner,), device_id_type=MESH)
+
+    def end_a(p):
+        for h in range(2):
+            step_a(p, h).wait()
+
+            def add(z, carry):
+                for i in range(2):
+                    if h:
+                        chunk(p, h)[core, z, yy, i] += ra[p, h, z, i]
+                    else:
+                        chunk(p, h)[core, z, i, xx] += ra[p, h, z, i]
+                return carry
+
+            lax.fori_loop(0, 4, add, 0)
+            step_b(p, h).start()
+
+    def end_b(p):
+        for h in range(2):
+            step_b(p, h).wait()
+
+            def add(z, carry):
+                chunk(p, h)[core, z, yy, xx] += rb[p, h, z]
+                return carry
+
+            lax.fori_loop(0, 4, add, 0)
+            for hop in range(1, 4):
+                step_z(p, h, hop).start()
+
+    def end_z(p):
+        for h in range(2):
+            for hop in range(1, 4):
+                step_z(p, h, hop).wait()
+            total = chunk(p, h)[core, zz, yy, xx].astype(F32)
+            for hop in range(3):
+                total += rz[p, h, hop].astype(F32)
+            at = 384 * h
+            if p < 2:
+                wbg[48 * p:48 * p + 48, at:at + 384] = total
+                continue
+            if p < 4:
+                low_ref, high_ref, at, up = wig, wig, (p - 2) * 1536 + at, D
+            elif p == 4:
+                low_ref, high_ref, up = wvg, wog, 0
+            else:
+                low_ref, high_ref, up = wqg, wkg, 0
+            low_ref[:, at:at + 384] = total[0:24]
+            high_ref[:, at + up:at + up + 384] = total[24:48]
+
+    def store_grad(p, t, i, grad):
+        for h in range(2):
+            chunk(p, h)[i % 2, t, i // 4, (i // 2) % 2] = grad[:, 384 * h:384 * h + 384]
 
     for h in range(2):
         def back_grad(t, carry):
@@ -863,11 +877,13 @@
             )
             grad = dot_nn(left, ml[...]).astype(BF16)
             for i in range(8):
-                chunk(h)[i % 2, t, i // 4, (i // 2) % 2] = grad[48 * i:48 * i + 48]
+                store_grad(h, t, i, grad[48 * i:48 * i + 48])
             return carry
 
         lax.fori_loop(0, 4, back_grad, 0)
         start_c(h)
+        if h == 1:
+            end_c(0)
 
     for t in range(4):
         cols = pl.ds(t * D, D)
@@ -883,9 +899,9 @@
         vec[8 + t:9 + t, :] = jnp.sum(total, axis=0, keepdims=True)
         n2[...] += dot_nt(gp[:, cols], wi[:, cols])
         if t == 0:
-            end_c(0)
-        if t == 1:
             end_c(1)
+        if t == 2:
+            end_a(0)
 
     def pair_grad(k, left_0, right_0, left_1, right_1):
         def group(t, carry):
@@ -894,17 +910,20 @@
             grad_1 = dot_nn(left_1[rows, :], right_1[...]).reshape(8, 24, D)
             both = jnp.concatenate([grad_0, grad_1], axis=1).astype(BF16)
             for i in range(8):
-                chunk(k)[i % 2, t, i // 4, (i // 2) % 2] = both[i]
+                store_grad(k, t, i, both[i])
             return carry
 
         lax.fori_loop(0, 4, group, 0)
         start_c(k)
 
     for j in range(2):
+        if j == 1:
+            end_c(2)
         pair_grad(2 + j, mlT, gp.at[:, pl.ds(2 * j * D, D)], mlT, gp.at[:, pl.ds((2 * j + 1) * D, D)])
 
+    end_a(1)
     def attn_norm_back(i, sums):
-        rows = pl.ds(pl.multiple_of(i * 16, 16), 16)
+        rows = pl.ds(pl.multiple_of(i * 32, 16), 32)
         upstream, unit = n2[rows, :], n1[rows, :]
         scaled = upstream * gain1
         hidden_grad = r1[rows, :] * (
@@ -919,13 +938,12 @@
             sums[0] + fold8(upstream * unit), sums[1] + fold8(upstream), sums[2] + fold8(rounded.astype(F32)),
         )
 
-    sums = lax.fori_loop(0, 30, attn_norm_back, (zero8, zero8, zero8))
+    sums = lax.fori_loop(0, 15, attn_norm_back, (zero8, zero8, zero8))
     vec[2:3, :] = jnp.sum(sums[2], axis=0, keepdims=True)
     vec[3:4, :] = jnp.sum(sums[0], axis=0, keepdims=True)
     vec[4:5, :] = jnp.sum(sums[1], axis=0, keepdims=True)
+    end_c(3)
     c_s[...] = dot_nt(ml[...], wo[...]).astype(BF16)
-    end_c(2)
-    end_c(3)
 
     q_rows, k_rows, v_rows = spread(q_s[0:32, :]), k_s[0:32, :], v_s[0:32, :]
     dc_rows = spread(c_s[0:32, :])
@@ -968,10 +986,12 @@
                     ref[256:480, lanes] = new[16:240].astype(BF16)
         return carry
 
-    lax.fori_loop(0, 3, attend_back, 0)
-    end_a(0)
-    end_a(1)
-    lax.fori_loop(3, 6, attend_back, 0)
+    lax.fori_loop(0, 2, attend_back, 0)
+    end_b(0)
+    lax.fori_loop(2, 4, attend_back, 0)
+    end_a(2)
+    lax.fori_loop(4, 6, attend_back, 0)
+    end_b(1)
 
     def column_sum(ref):
         def step(i, total):
@@ -981,60 +1001,52 @@
 
     vec[0:1, :] = column_sum(q_s)
     vec[1:2, :] = column_sum(v_s)
-    end_b(0)
-    end_b(1)
-    pair_grad(4, xT, v_s, cT, ml)
-    pair_grad(5, xT, q_s, xT, k_s)
-
     def vec_step(i, device):
         return remote(vec, vecr.at[i], v_send.at[i], v_recv.at[i], device)
-
-    vec_step(0, partner).start()
-    end_c(4)
-    end_c(5)
-    n1[...] += dot_nt(q_s[...], wq[...])
-    vec_step(0, partner).wait()
-    vec[...] += vecr[0]
-    vec_step(1, x_peer).start()
-    n1[...] += dot_nt(k_s[...], wk[...])
-    vec_step(1, x_peer).wait()
-    vec[...] += vecr[1]
-    vec_step(2, y_peer).start()
-    n1[...] += dot_nt(v_s[...], wv[...])
-    vec_step(2, y_peer).wait()
-    vec[...] += vecr[2]
 
     def vec_z(hop):
         return remote(
             vec, vecz.at[hop - 1], v_send.at[2 + hop], v_recv.at[2 + hop], lax.rem(zz + hop, 4) * 8 + plane
         )
 
-    for hop in range(1, 4):
-        vec_z(hop).start()
+    vec_step(0, partner).start()
+    pair_grad(4, xT, v_s, cT, ml)
+    pair_grad(5, xT, q_s, xT, k_s)
+    vec_step(0, partner).wait()
+    vec[...] += vecr[0]
+    vec_step(1, x_peer).start()
+    end_a(3)
+    end_c(4)
+    n1[...] += dot_nt(q_s[...], wq[...])
+    end_c(5)
+    end_b(2)
+    vec_step(1, x_peer).wait()
+    vec[...] += vecr[1]
+    vec_step(2, y_peer).start()
+    n1[...] += dot_nt(k_s[...], wk[...])
+    n1[...] += dot_nt(v_s[...], wv[...])
     out_qg = pltpu.make_async_copy(n1.at[0:32, :], qtg_h, out_sem.at[2])
     out_pg = pltpu.make_async_copy(n1.at[32:472, :], ptg_h, out_sem.at[3])
     out_qg.start()
     out_pg.start()
     end_z(0)
     end_z(1)
+    vec_step(2, y_peer).wait()
+    vec[...] += vecr[2]
+    for hop in range(1, 4):
+        vec_z(hop).start()
+    end_a(4)
+    end_b(3)
+    end_z(2)
     for hop in range(1, 4):
         vec_z(hop).wait()
     whole = vec[...] + vecz[0] + vecz[1] + vecz[2]
-    small = pltpu.roll(whole, D - 24 * me, 1)
-    for at, ref in enumerate((bqg, bvg, bog, gag, sag, bbg, gfg, sfg)):
-        ref[...] = small[at:at + 1, 0:24]
+    small_o[0:8, :] = pltpu.roll(whole[0:8], D - 24 * me, 1)[:, 0:128]
     wide = pltpu.roll(whole[8:16], D - 96 * plane, 1)
-    big[...] = jnp.sum(jnp.where(iota((8, D), 0) == zz, wide, 0.0), axis=0, keepdims=True)[:, 0:96]
-
-    end_a(2)
-    end_a(3)
-    end_b(2)
-    end_b(3)
-    end_a(4)
+    small_o[8:9, :] = jnp.sum(jnp.where(iota((8, D), 0) == zz, wide, 0.0), axis=0, keepdims=True)[:, 0:128]
     end_a(5)
-    end_z(2)
+    end_b(4)
     end_z(3)
-    end_b(4)
     end_b(5)
     end_z(4)
     end_z(5)
@@ -1042,6 +1054,26 @@
     out_p.wait()
     out_qg.wait()
     out_pg.wait()
+
+
+def hand_on_kernel(*refs):
+    count = 10
+    sources, small = refs[:count], refs[count]
+    targets, vectors = refs[count + 1:2 * count + 1], refs[2 * count + 1:2 * count + 11]
+    held, in_sem, out_sem = refs[2 * count + 11:3 * count + 11], refs[-2], refs[-1]
+    into = [pltpu.make_async_copy(sources[i], held[i], in_sem.at[i]) for i in range(count)]
+    out = [pltpu.make_async_copy(held[i], targets[i], out_sem.at[i]) for i in range(count)]
+    for copy in into:
+        copy.start()
+    for at, ref in enumerate(vectors[:8]):
+        ref[...] = small[at:at + 1, 0:24].reshape(24)
+    vectors[8][...] = small[8:9, 0:96].reshape(96)
+    vectors[9][...] = small[9:10, 0:1].reshape(1)
+    for first, second in zip(into, out):
+        first.wait()
+        second.start()
+    for copy in out:
+        copy.wait()
 
 
 def on_device_small(*operands):
@@ -1053,23 +1085,23 @@
     hbm, vmem, smem = (pl.BlockSpec(memory_space=space) for space in (pl.ANY, pltpu.VMEM, pltpu.SMEM))
     shape = jax.ShapeDtypeStruct
     slabs = (2, 2, 4, 2, 2, 48, D)
+    large = (
+        shape((32, D), BF16), shape((440, D), BF16), shape((32, D), F32), shape((440, D), F32), shape((24, D), F32),
+        shape((24, D), F32), shape((24, D), F32), shape((24, D), F32), shape((24, FF), F32), shape((96, D), F32),
+    )
     outs = pl.pallas_call(
         layer_kernel,
         out_shape=(
-            shape((32, D), BF16), shape((440, D), BF16), shape((1, 1), F32), shape((32, D), F32), shape((440, D), F32),
-            shape((24, D), F32), shape((1, 24), F32), shape((24, D), F32), shape((24, D), F32), shape((1, 24), F32),
-            shape((24, D), F32), shape((1, 24), F32), shape((1, 24), F32), shape((1, 24), F32),
-            shape((24, FF), F32), shape((1, 96), F32), shape((96, D), F32), shape((1, 24), F32), shape((1, 24), F32),
-            shape((1, 24), F32),
+            *large, shape((16, 128), F32),
         ),
         in_specs=[
             hbm, hbm, smem, smem, smem, smem, smem, smem, hbm, hbm,
             hbm, vmem, hbm, hbm, vmem, hbm, vmem, vmem, vmem, hbm, vmem, hbm, vmem, vmem, vmem,
         ],
-        out_specs=(hbm, hbm, vmem, hbm, hbm) + (vmem,) * 15,
+        out_specs=(hbm,) * 4 + (vmem,) * 7,
         scratch_shapes=[
             pltpu.VMEM((D, D), BF16), pltpu.VMEM((D, D), BF16), pltpu.VMEM((D, D), BF16), pltpu.VMEM((D, D), BF16),
-            pltpu.VMEM((D, FF), BF16), pltpu.VMEM(slabs, BF16),
+            pltpu.VMEM((D, FF), BF16), pltpu.VMEM((2, 2, 2, 4, 2, 2, 48, 384), BF16),
             pltpu.VMEM((440, D), BF16), pltpu.VMEM((ROWS, D), BF16), pltpu.VMEM((D, ROWS), BF16),
             pltpu.VMEM((ROWS, D), BF16), pltpu.VMEM((ROWS, D), BF16), pltpu.VMEM((ROWS, D), BF16),
             pltpu.VMEM((2, 12, WIN, WIN), BF16), pltpu.VMEM((32, 384), BF16),
@@ -1081,15 +1113,15 @@
             pltpu.VMEM((32, D), BF16), pltpu.VMEM((440, D), BF16), pltpu.VMEM((32, D), BF16), pltpu.VMEM((440, D), BF16),
             pltpu.VMEM((768, 128), F32), pltpu.VMEM((8, D), F32),
             pltpu.VMEM((16, D), F32), pltpu.VMEM((3, 16, D), F32), pltpu.VMEM((3, 16, D), F32),
-            pltpu.VMEM((4, 2, 4, 2, 2, 48, D), BF16),
-            pltpu.VMEM((2, 4, 2, 2, 48, D), BF16), pltpu.VMEM((6, 4, 2, 48, D), BF16), pltpu.VMEM((6, 4, 48, D), BF16),
-            pltpu.VMEM((6, 3, 48, D), BF16),
-            pltpu.SemaphoreType.DMA((10,)), pltpu.SemaphoreType.DMA((4,)),
+            pltpu.VMEM((4, 2, 2, 4, 2, 2, 48, 384), BF16),
+            pltpu.VMEM((2, 2, 4, 2, 2, 48, 384), BF16), pltpu.VMEM((6, 2, 4, 2, 48, 384), BF16),
+            pltpu.VMEM((6, 2, 4, 48, 384), BF16), pltpu.VMEM((6, 2, 3, 48, 384), BF16),
+            pltpu.SemaphoreType.DMA((12,)), pltpu.SemaphoreType.DMA((4,)),
             pltpu.SemaphoreType.DMA((16,)), pltpu.SemaphoreType.DMA((16,)),
-            pltpu.SemaphoreType.DMA((6,)), pltpu.SemaphoreType.DMA((6,)),
-            pltpu.SemaphoreType.DMA((6,)), pltpu.SemaphoreType.DMA((6,)),
-            pltpu.SemaphoreType.DMA((6,)), pltpu.SemaphoreType.DMA((6,)),
-            pltpu.SemaphoreType.DMA((6, 3)), pltpu.SemaphoreType.DMA((6, 3)),
+            pltpu.SemaphoreType.DMA((6, 2)), pltpu.SemaphoreType.DMA((6, 2)),
+            pltpu.SemaphoreType.DMA((6, 2)), pltpu.SemaphoreType.DMA((6, 2)),
+            pltpu.SemaphoreType.DMA((6, 2)), pltpu.SemaphoreType.DMA((6, 2)),
+            pltpu.SemaphoreType.DMA((6, 2, 3)), pltpu.SemaphoreType.DMA((6, 2, 3)),
             pltpu.SemaphoreType.DMA((6,)), pltpu.SemaphoreType.DMA((6,)),
             pltpu.SemaphoreType.REGULAR,
         ],
@@ -1103,8 +1135,19 @@
         weight_out, bias_out, gain_attn, shift_attn, weight_in, bias_in, weight_back.reshape(slabs), bias_back,
         gain_ffn, shift_ffn,
     )
-    flat = lambda array: array.reshape(-1)
-    return tuple(flat(out) if out.shape[0] == 1 else out for out in outs)
+    done = pl.pallas_call(
+        hand_on_kernel,
+        out_shape=large + (shape((24,), F32),) * 8 + (shape((96,), F32), shape((1,), F32)),
+        in_specs=[hbm] * 10 + [vmem],
+        out_specs=(hbm,) * 10 + (vmem,) * 10,
+        scratch_shapes=[pltpu.VMEM(out.shape, out.dtype) for out in large]
+        + [pltpu.SemaphoreType.DMA((10,)), pltpu.SemaphoreType.DMA((10,))],
+        name="hand_on",
+    )(*outs)
+    qout, pout, qtg, ptg, wqg, wkg, wvg, wog, wig, wbg, bqg, bvg, bog, gag, sag, bbg, gfg, sfg, big, loss = done
+    return (
+        qout, pout, loss, qtg, ptg, wqg, bqg, wkg, wvg, bvg, wog, bog, gag, sag, wig, big, wbg, bbg, gfg, sfg,
+    )
 
 
 def solution(mesh):

time: 170 us -> 131 us (0.77)
  Pallas kernels: 150 us -> 127 us
  local copies, waits for them, and re-layouts: 13.9 us -> 0 us
    pallas_call x1 -> x2, Pallas kernels: 150 us -> 127 us  [the longest x1 123 us: on_device_small(): pl.pallas_call(layer_kernel, out_shape=(*large, shape((16, 128), F32)), i...]
    unnamed x53 -> x0, local copies, waits for them, and re-layouts: 13.9 us -> none
where the time goes in v2:
time: 131 us
  Pallas kernels  127 us (97%)
  between operations  3.41 us (3%)
    pallas_call x1, Pallas kernels, on_device_small(): pl.pallas_call(layer_kernel, out_shape=(*large, shape((16, 128), F32)), i...  123 us
    pallas_call x1, Pallas kernels, on_device_small(): pl.pallas_call(hand_on_kernel, out_shape=large + (shape((24,), F32),) * 8...  4.42 us

profile of v2, /device:TPU:0, one launch (start us, length us, event | category | flops | bytes accessed | tf_op | source)
XLA Modules:
  0.0 130.5 jit_solution(14783795918963404656)
XLA Ops:
  3.2 122.7 %encoder_layer.1 = (bf16[32,768]{1,0:T(8,128)(2,1)}, bf16[440,768]{1,0:T(8,128)(2,1)}, f32[32,768]{1,0:T(8,128)}, f32[440,768]{1,0:T(8,128)}, f32[24,768]{1,0:T(...) custom-call(bf16[32,768]{1,0:T(8,128)(2,1)} %qtok.1, ...), custom_call_target="tpu_custom_call" | custom-call | tf_op jit(solution)/shard_map/encoder_layer/pallas_call | solution.py:1092
  125.9 4.4 %hand_on.1 = (bf16[32,768]{1,0:T(8,128)(2,1)}, bf16[440,768]{1,0:T(8,128)(2,1)}, f32[32,768]{1,0:T(8,128)}, f32[440,768]{1,0:T(8,128)}, f32[24,768]{1,0:T(8,128)...) custom-call(bf16[32,768]{1,0:T(8,128)(2,1)} %get-tuple-element.51.re, ...), custom_call_target="tpu_custom_call" | custom-call | tf_op jit(solution)/shard_map/hand_on/pallas_call | solution.py:1138

commit v3 on v2

--- a/solution.py
+++ b/solution.py
@@ -459,6 +459,10 @@
     return ref[pl.ds(start, size)].astype(F32).reshape(1, size)
 
 
+def blocks(start, stop, size):
+    return [(at, min(size, stop - at)) for at in range(start, stop, size)]
+
+
 def iota(shape, dim):
     return lax.broadcasted_iota(jnp.int32, shape, dim)
 
@@ -467,13 +471,31 @@
     return jnp.sum(block.reshape(-1, 8, block.shape[-1]), axis=0)
 
 
+Z_FIRST = (1, 1)
+ORDER = (
+    ("wback", 0), ("c", 0, 0), ("c", 0, 1), ("wback", 1), ("c", 1, 0), ("ec", 0, 0), ("c", 1, 1), ("dinner", 0),
+    ("ec", 0, 1), ("dinner", 1), ("win", 2, (0, 1)), ("win", 2, (2, 3)), ("c", 2, 0), ("ec", 1, 0), ("c", 2, 1),
+    ("dinner", 2), ("dinner", 3), ("ec", 1, 1), ("win", 3, (0, 1)), ("e1", 0, 0), ("ec", 2, 1), ("win", 3, (2, 3)),
+    ("c", 3, 0), ("ec", 2, 0), ("c", 3, 1), ("dmid", 0), ("dmid", 1), ("dmid", 2), ("dmid", 3), ("ec", 3, 1),
+    ("lnback",), ("ec", 3, 0), ("dctx",), ("e1", 0, 1), ("e2", 0, 0), ("qslot",), ("attn", 0), ("attn", 1),
+    ("attn", 2), ("e1", 1, 0), ("attn", 3), ("attn", 4), ("attn", 5), ("e1", 3, 0), ("sums",), ("vec", 0),
+    ("wvo", (0, 1)), ("e1", 3, 1), ("wvo", (2, 3)), ("c", 4, 0), ("e2", 1, 0), ("vec", 1), ("e1", 2, 0), ("c", 4, 1),
+    ("wqk", (0, 1)), ("e3", 0, 0), ("e2", 0, 1), ("vec", 2), ("e1", 2, 1), ("wqk", (2, 3)), ("ec", 4, 1),
+    ("e2", 3, 0), ("vec", 3), ("c", 5, 0), ("ec", 4, 0), ("e2", 3, 1), ("c", 5, 1), ("tq",), ("ec", 5, 1),
+    ("e2", 2, 1), ("vecend",), ("e3", 1, 0), ("e1", 4, 1), ("ec", 5, 0), ("e1", 4, 0), ("tk",), ("e2", 4, 1),
+    ("e2", 2, 0), ("e3", 0, 1), ("e3", 2, 1), ("e3", 4, 1), ("e1", 5, 1), ("e2", 4, 0), ("tv",), ("tout",),
+    ("e1", 1, 1), ("e1", 5, 0), ("e2", 1, 1), ("e2", 5, 1), ("e3", 3, 0), ("e2", 5, 0), ("e3", 1, 1), ("e3", 5, 1),
+    ("e3", 3, 1), ("e3", 2, 0), ("e3", 4, 0), ("e3", 5, 0),
+)
+
+
 def layer_kernel(
     qtok, ptok, qlen, plen, pvalid, pos, neg, margin, qgrad, pgrad,
-    wq_h, bq, wk_h, wv_h, bv, wo_h, bo, ga, sa, wi_h, bi, wb_h, bb, gf, sf,
+    wq_h, bq_h, wk_h, wv_h, bv_h, wo_h, bo_h, ga_h, sa_h, wi_h, bi_h, wb_h, bb_h, gf_h, sf_h,
     qout_h, pout_h, qtg_h, ptg_h, wqg, wkg, wvg, wog, wig, wbg, small_o,
-    wq, wk, wv, wo, wi, wb, pstage, x_s, xT, q_s, k_s, v_s, p_s, pq_s, c_s, cT, n1, n2, r1, r2,
-    ml, mlT, act_s, actT, tmp, gp, qg_s, pg_s, qo_s, po_s, ex, dcls, vec, vecr, vecz,
-    g_s, rc, ra, rb, rz,
+    bq, bv, bo, ga, sa, bi, bb, gf, sf, wq, wk, wv, wo, wi, wb, pstage, x_s, xT, q_s, k_s, v_s, p_s, pq_s, c_s, cT, n1, n2, r1, r2,
+    ml, mlT, act_a, act_b, actT, tmp_a, tmp_b, gp, qg_s, pg_s, qo_s, po_s, ex, dcls, vec, vecr, vecz,
+    g_s, rc, ra, rb, rz, rw,
     load_sem, out_sem, ex_send, ex_recv, c_send, c_recv, a_send, a_recv, b_send, b_recv,
     z_send, z_recv, v_send, v_recv, credit,
 ):
@@ -499,6 +521,9 @@
     load("wq", wq_h, wq)
     load("wk", wk_h, wk)
     load("wv", wv_h, wv)
+    vectors = ((bq_h, bq), (bv_h, bv), (bo_h, bo), (ga_h, ga), (sa_h, sa), (bi_h, bi), (bb_h, bb), (gf_h, gf), (sf_h, sf))
+    for at, (source, target) in enumerate(vectors):
+        load("vec" + str(at), source, target)
 
     barrier = pltpu.get_barrier_semaphore()
     for hop in range(1, 16):
@@ -520,6 +545,8 @@
     ).astype(BF16)
 
     loads["wq"].wait()
+    for at in range(len(vectors)):
+        loads["vec" + str(at)].wait()
     load("wo", wo_h, wo)
     load("wi", wi_h, wi)
     q_s[...] = ((dot_nn(x_s[...], wq[...]) + row_of(bq)).astype(BF16) * 0.125).astype(BF16)
@@ -579,69 +606,69 @@
     lax.fori_loop(0, 6, attend, 0)
 
     loads["wo"].wait()
-    tmp[...] = dot_nn(c_s[...], wo[...])
     gain1, shift1, bias1 = row_of(ga), row_of(sa), row_of(bo)
-
-    def norm_attn(i, carry):
-        rows = pl.ds(pl.multiple_of(i * 48, 16), 48)
-        hidden = tmp[rows, :] + x_s[rows, :].astype(F32) + bias1
+    gain2, shift2, bias2 = row_of(gf), row_of(sf), row_of(bb)
+
+    def wb_tile(t):
+        return jnp.concatenate([wb[h, t // 2, t % 2].reshape(D, 384) for h in range(2)], axis=1)
+
+    def normalized(hidden):
         centered = hidden - jnp.mean(hidden, axis=-1, keepdims=True)
         inv = lax.rsqrt(jnp.mean(centered * centered, axis=-1, keepdims=True) + ln_eps)
-        unit = centered * inv
-        n1[rows, :] = unit
-        r1[rows, :] = inv
-        ml[rows, :] = (unit * gain1 + shift1).astype(BF16)
-        return carry
-
-    lax.fori_loop(0, 10, norm_attn, 0)
-
-    loads["wi"].wait()
-    loads["wb0"].wait()
-    loads["wb1"].wait()
-
-    def wb_tile(t):
-        return jnp.concatenate([wb[h, t // 2, t % 2].reshape(D, 384) for h in range(2)], axis=1)
-
-    for t in range(4):
-        cols = pl.ds(t * D, D)
-        tmp[...] = dot_nn(ml[...], wi[:, cols])
-        bias_t = row_of(bi, t * D)
-
-        def activate(i, carry):
-            rows = pl.ds(pl.multiple_of(i * 16, 16), 16)
-            u = tmp[rows, :] + bias_t
-            cdf = 0.5 * (1.0 + lax.erf(u * root_half))
-            act_s[rows, :] = (u * cdf).astype(BF16)
-            gp[rows, cols] = (cdf + u * inv_root_tau * jnp.exp(-0.5 * u * u)).astype(BF16)
-            return carry
-
-        lax.fori_loop(0, 30, activate, 0)
-        if t == 0:
-            n2[...] = dot_nn(act_s[...], wb_tile(t))
-        else:
-            n2[...] += dot_nn(act_s[...], wb_tile(t))
-        actT[cols, :] = act_s[...].T
-
-    gain2, shift2, bias2 = row_of(gf), row_of(sf), row_of(bb)
-
-    def norm_ffn_at(r0, size):
-        rows = pl.ds(r0, size)
-        hidden = n2[rows, :] + (n1[rows, :] * gain1 + shift1) + bias2
-        centered = hidden - jnp.mean(hidden, axis=-1, keepdims=True)
-        inv = lax.rsqrt(jnp.mean(centered * centered, axis=-1, keepdims=True) + ln_eps)
-        unit = centered * inv
-        n2[rows, :] = unit
-        r2[rows, :] = inv
-        return (unit * gain2 + shift2).astype(BF16)
-
-    qo_s[...] = norm_ffn_at(0, 32)
-
-    def norm_ffn(i, carry):
-        po_s[pl.ds(pl.multiple_of(i * 48, 16), 48), :] = norm_ffn_at(pl.multiple_of(32 + i * 48, 16), 48)
-        return carry
-
-    lax.fori_loop(0, 9, norm_ffn, 0)
-    po_s[432:440, :] = norm_ffn_at(464, 16)[0:8]
+        return centered * inv, inv
+
+    def forward_rows(start, stop):
+        size = stop - start
+        every, own = pl.ds(start, size), pl.ds(0, size)
+        tmp_a[own, :] = dot_nn(c_s[every, :], wo[...])
+        for at, count in blocks(0, size, 32):
+            rows, here = pl.ds(start + at, count), pl.ds(at, count)
+            unit, inv = normalized(tmp_a[here, :] + x_s[rows, :].astype(F32) + bias1)
+            n1[rows, :] = unit
+            r1[rows, :] = inv
+            ml[rows, :] = (unit * gain1 + shift1).astype(BF16)
+        if start == 0:
+            loads["wi"].wait()
+            loads["wb0"].wait()
+            loads["wb1"].wait()
+        inner, acts = (tmp_a, tmp_b), (act_a, act_b)
+        tmp_a[own, :] = dot_nn(ml[every, :], wi[:, 0:D])
+
+        def finish(t):
+            act = acts[t % 2][own, :]
+            if t == 0:
+                n2[every, :] = dot_nn(act, wb_tile(t))
+            else:
+                n2[every, :] += dot_nn(act, wb_tile(t))
+            actT[t * D:t * D + D, every] = act.T
+
+        for t in range(4):
+            if t < 3:
+                inner[(t + 1) % 2][own, :] = dot_nn(ml[every, :], wi[:, t * D + D:t * D + 2 * D])
+            bias_t = row_of(bi, t * D)
+            for at, count in blocks(0, size, 16):
+                here = pl.ds(at, count)
+                u = inner[t % 2][here, :] + bias_t
+                cdf = 0.5 * (1.0 + lax.erf(u * root_half))
+                acts[t % 2][here, :] = (u * cdf).astype(BF16)
+                gp[start + at:start + at + count, t * D:t * D + D] = (
+                    cdf + u * inv_root_tau * jnp.exp(-0.5 * u * u)
+                ).astype(BF16)
+            if t > 0:
+                finish(t - 1)
+        finish(3)
+        for at, count in blocks(start, stop, 32):
+            rows = pl.ds(at, count)
+            unit, inv = normalized(n2[rows, :] + (n1[rows, :] * gain1 + shift1) + bias2)
+            n2[rows, :] = unit
+            r2[rows, :] = inv
+            out = (unit * gain2 + shift2).astype(BF16)
+            if at == 0:
+                qo_s[...] = out
+            else:
+                po_s[at - 32:min(at, 440), :] = out[0:min(count, 472 - at)]
+
+    forward_rows(0, 256)
 
     slot_me = core * 16 + chip
     base = pl.multiple_of(slot_me * 24, 8)
@@ -669,14 +696,12 @@
         ))
         sends[-1].start()
 
+    forward_rows(256, 480)
     out_q = pltpu.make_async_copy(qo_s, qout_h, out_sem.at[0])
     out_p = pltpu.make_async_copy(po_s, pout_h, out_sem.at[1])
     out_q.start()
     out_p.start()
-
     mlT[...] = ml[...].T
-    xT[...] = x_s[...].T
-    cT[...] = c_s[...].T
     loads["qg"].wait()
     loads["pg"].wait()
 
@@ -696,14 +721,10 @@
             sums[0] + fold8(upstream * unit), sums[1] + fold8(upstream), sums[2] + fold8(rounded.astype(F32)),
         )
 
-    def middle_block(i, sums):
-        upstream = pg_s[pl.ds(pl.multiple_of(i * 32, 16), 32), :].astype(F32)
-        return ffn_norm_back(pl.multiple_of(32 + i * 32, 16), upstream, sums)
-
     zero8 = jnp.zeros((8, D), F32)
     sums = (zero8, zero8, zero8)
-    sums = lax.fori_loop(1, 6, middle_block, sums)
-    sums = lax.fori_loop(7, 13, middle_block, sums)
+    for i in (1, 2, 3, 4, 5, 7, 8, 9, 10, 11, 12):
+        sums = ffn_norm_back(32 + 32 * i, pg_s[32 * i:32 * i + 32, :].astype(F32), sums)
     last = jnp.concatenate([pg_s[416:440, :].astype(F32), jnp.zeros((8, D), F32)], axis=0)
     sums = ffn_norm_back(448, last, sums)
 
@@ -715,6 +736,8 @@
         device_id=(partner,), device_id_type=MESH,
     )
     across.start()
+    xT[...] = x_s[...].T
+    cT[...] = c_s[...].T
     across.wait()
 
     def first(r):
@@ -775,188 +798,216 @@
     def chunk(p, h):
         return g_s.at[p, h] if p < 4 else wb.at[h, p - 4]
 
+    def route(p, h):
+        return "zyx" if (p, h) == Z_FIRST else ("xyz", "yxz")[h]
+
     def remote(source, target, send, recv, device):
         return pltpu.make_async_remote_copy(
             src_ref=source, dst_ref=target, send_sem=send, recv_sem=recv, device_id=(device,), device_id_type=MESH,
         )
 
     def step_c(p, h):
-        return remote(chunk(p, h).at[1 - core], rc.at[p % 2, h], c_send.at[p, h], c_recv.at[p, h], partner)
-
-    def step_a(p, h):
-        away = chunk(p, h).at[core, :, 1 - yy] if h else chunk(p, h).at[core, :, :, 1 - xx]
-        return remote(away, ra.at[p, h], a_send.at[p, h], a_recv.at[p, h], y_peer if h else x_peer)
-
-    def step_b(p, h):
-        away = chunk(p, h).at[core, :, yy, 1 - xx] if h else chunk(p, h).at[core, :, 1 - yy, xx]
-        return remote(away, rb.at[p, h], b_send.at[p, h], b_recv.at[p, h], x_peer if h else y_peer)
-
-    def step_z(p, h, hop):
-        to = lax.rem(zz + hop, 4)
-        return remote(
-            chunk(p, h).at[core, to, yy, xx], rz.at[p, h, hop - 1], z_send.at[p, h, hop - 1], z_recv.at[p, h, hop - 1],
-            to * 8 + plane,
-        )
-
-    def start_c(p):
-        for h in range(2):
-            if p >= 2:
-                pl.semaphore_wait(credit, 1)
-            step_c(p, h).start()
-
-    def end_c(p):
-        for h in range(2):
-            step_c(p, h).wait()
-
-            def add(z, carry):
-                for y in range(2):
-                    for x in range(2):
-                        chunk(p, h)[core, z, y, x] += rc[p % 2, h, z, y, x]
+        return [remote(chunk(p, h).at[1 - core], rc.at[p % 2, h], c_send.at[p, h], c_recv.at[p, h], partner)]
+
+    def along_z(p, h, pick, target):
+        steps = []
+        for hop in range(1, 4):
+            to = lax.rem(zz + hop, 4)
+            steps.append(remote(
+                pick(to), target(hop - 1), z_send.at[p, h, hop - 1], z_recv.at[p, h, hop - 1], to * 8 + plane,
+            ))
+        return steps
+
+    def step_1(p, h):
+        mine, way = chunk(p, h), route(p, h)
+        if way == "zyx":
+            return along_z(p, h, lambda to: mine.at[core, to], lambda i: rw.at[i])
+        away = mine.at[core, :, :, 1 - xx] if way == "xyz" else mine.at[core, :, 1 - yy]
+        return [remote(away, ra.at[p, h], a_send.at[p, h], a_recv.at[p, h], x_peer if way == "xyz" else y_peer)]
+
+    def step_2(p, h):
+        mine, way = chunk(p, h), route(p, h)
+        if way == "zyx":
+            away, target = mine.at[core, zz, 1 - yy], rb.at[p, h, 0:2]
+        elif way == "xyz":
+            away, target = mine.at[core, :, 1 - yy, xx], rb.at[p, h]
+        else:
+            away, target = mine.at[core, :, yy, 1 - xx], rb.at[p, h]
+        return [remote(away, target, b_send.at[p, h], b_recv.at[p, h], x_peer if way == "yxz" else y_peer)]
+
+    def step_3(p, h):
+        mine = chunk(p, h)
+        if route(p, h) == "zyx":
+            return [remote(
+                mine.at[core, zz, yy, 1 - xx], rz.at[p, h, 0], a_send.at[p, h], a_recv.at[p, h], x_peer,
+            )]
+        return along_z(p, h, lambda to: mine.at[core, to, yy, xx], lambda i: rz.at[p, h, i])
+
+    def begin(steps):
+        for step in steps:
+            step.start()
+
+    def finish_steps(steps):
+        for step in steps:
+            step.wait()
+
+    def start_c(p, h):
+        if p >= 2:
+            pl.semaphore_wait(credit.at[p % 2, h], 1)
+        begin(step_c(p, h))
+
+    def end_c(p, h):
+        finish_steps(step_c(p, h))
+
+        def add(z, carry):
+            for y in range(2):
+                for x in range(2):
+                    chunk(p, h)[core, z, y, x] += rc[p % 2, h, z, y, x]
+            return carry
+
+        lax.fori_loop(0, 4, add, 0)
+        begin(step_1(p, h))
+        if p < 4:
+            pl.semaphore_signal(credit.at[p % 2, h], inc=1, device_id=(partner,), device_id_type=MESH)
+
+    def end_1(p, h):
+        finish_steps(step_1(p, h))
+        mine, way = chunk(p, h), route(p, h)
+        if way == "zyx":
+            def add(y, carry):
+                for x in range(2):
+                    total = mine[core, zz, y, x].astype(F32)
+                    for i in range(3):
+                        total += rw[i, y, x].astype(F32)
+                    mine[core, zz, y, x] = total.astype(BF16)
                 return carry
 
-            lax.fori_loop(0, 4, add, 0)
-            step_a(p, h).start()
-            if p < 4:
-                pl.semaphore_signal(credit, inc=1, device_id=(partner,), device_id_type=MESH)
-
-    def end_a(p):
-        for h in range(2):
-            step_a(p, h).wait()
-
+            lax.fori_loop(0, 2, add, 0)
+        else:
             def add(z, carry):
                 for i in range(2):
-                    if h:
-                        chunk(p, h)[core, z, yy, i] += ra[p, h, z, i]
+                    if way == "yxz":
+                        mine[core, z, yy, i] += ra[p, h, z, i]
                     else:
-                        chunk(p, h)[core, z, i, xx] += ra[p, h, z, i]
+                        mine[core, z, i, xx] += ra[p, h, z, i]
                 return carry
 
             lax.fori_loop(0, 4, add, 0)
-            step_b(p, h).start()
-
-    def end_b(p):
-        for h in range(2):
-            step_b(p, h).wait()
-
+        begin(step_2(p, h))
+
+    def end_2(p, h):
+        finish_steps(step_2(p, h))
+        mine = chunk(p, h)
+        if route(p, h) == "zyx":
+            for x in range(2):
+                mine[core, zz, yy, x] += rb[p, h, x]
+        else:
             def add(z, carry):
-                chunk(p, h)[core, z, yy, xx] += rb[p, h, z]
+                mine[core, z, yy, xx] += rb[p, h, z]
                 return carry
 
             lax.fori_loop(0, 4, add, 0)
-            for hop in range(1, 4):
-                step_z(p, h, hop).start()
-
-    def end_z(p):
-        for h in range(2):
-            for hop in range(1, 4):
-                step_z(p, h, hop).wait()
-            total = chunk(p, h)[core, zz, yy, xx].astype(F32)
-            for hop in range(3):
-                total += rz[p, h, hop].astype(F32)
-            at = 384 * h
-            if p < 2:
-                wbg[48 * p:48 * p + 48, at:at + 384] = total
-                continue
-            if p < 4:
-                low_ref, high_ref, at, up = wig, wig, (p - 2) * 1536 + at, D
-            elif p == 4:
-                low_ref, high_ref, up = wvg, wog, 0
-            else:
-                low_ref, high_ref, up = wqg, wkg, 0
-            low_ref[:, at:at + 384] = total[0:24]
-            high_ref[:, at + up:at + up + 384] = total[24:48]
+        begin(step_3(p, h))
+
+    def end_3(p, h):
+        finish_steps(step_3(p, h))
+        total = chunk(p, h)[core, zz, yy, xx].astype(F32)
+        for i in range(1 if route(p, h) == "zyx" else 3):
+            total += rz[p, h, i].astype(F32)
+        at = 384 * h
+        if p < 2:
+            wbg[48 * p:48 * p + 48, at:at + 384] = total
+            return
+        if p < 4:
+            low_ref, high_ref, at, up = wig, wig, (p - 2) * 1536 + at, D
+        elif p == 4:
+            low_ref, high_ref, up = wvg, wog, 0
+        else:
+            low_ref, high_ref, up = wqg, wkg, 0
+        low_ref[:, at:at + 384] = total[0:24]
+        high_ref[:, at + up:at + up + 384] = total[24:48]
 
     def store_grad(p, t, i, grad):
         for h in range(2):
             chunk(p, h)[i % 2, t, i // 4, (i // 2) % 2] = grad[:, 384 * h:384 * h + 384]
 
-    for h in range(2):
-        def back_grad(t, carry):
+    def back_grad(p):
+        for t in range(4):
             left = jnp.concatenate(
-                [actT[pl.ds(pl.multiple_of(t * D + 96 * i + 48 * h, 16), 48), :] for i in range(8)], axis=0
+                [actT[t * D + 96 * i + 48 * p:t * D + 96 * i + 48 * p + 48, :] for i in range(8)], axis=0
             )
             grad = dot_nn(left, ml[...]).astype(BF16)
             for i in range(8):
-                store_grad(h, t, i, grad[48 * i:48 * i + 48])
-            return carry
-
-        lax.fori_loop(0, 4, back_grad, 0)
-        start_c(h)
-        if h == 1:
-            end_c(0)
-
-    for t in range(4):
-        cols = pl.ds(t * D, D)
-        tmp[...] = dot_nt(ml[...], wb_tile(t))
-
-        def inner_back(i, total):
-            rows = pl.ds(pl.multiple_of(i * 16, 16), 16)
-            rounded = (tmp[rows, :] * gp[rows, cols].astype(F32)).astype(BF16)
-            gp[rows, cols] = rounded
-            return total + fold8(rounded.astype(F32))
-
-        total = lax.fori_loop(0, 30, inner_back, zero8)
-        vec[8 + t:9 + t, :] = jnp.sum(total, axis=0, keepdims=True)
-        n2[...] += dot_nt(gp[:, cols], wi[:, cols])
-        if t == 0:
-            end_c(1)
-        if t == 2:
-            end_a(0)
-
-    def pair_grad(k, left_0, right_0, left_1, right_1):
-        def group(t, carry):
-            rows = pl.ds(pl.multiple_of(t * 192, 16), 192)
+                store_grad(p, t, i, grad[48 * i:48 * i + 48])
+
+    def pair_grad(p, groups, left_0, right_0, left_1, right_1):
+        for t in groups:
+            rows = pl.ds(t * 192, 192)
             grad_0 = dot_nn(left_0[rows, :], right_0[...]).reshape(8, 24, D)
             grad_1 = dot_nn(left_1[rows, :], right_1[...]).reshape(8, 24, D)
             both = jnp.concatenate([grad_0, grad_1], axis=1).astype(BF16)
             for i in range(8):
-                store_grad(k, t, i, both[i])
-            return carry
-
-        lax.fori_loop(0, 4, group, 0)
-        start_c(k)
-
-    for j in range(2):
-        if j == 1:
-            end_c(2)
-        pair_grad(2 + j, mlT, gp.at[:, pl.ds(2 * j * D, D)], mlT, gp.at[:, pl.ds((2 * j + 1) * D, D)])
-
-    end_a(1)
-    def attn_norm_back(i, sums):
-        rows = pl.ds(pl.multiple_of(i * 32, 16), 32)
-        upstream, unit = n2[rows, :], n1[rows, :]
-        scaled = upstream * gain1
-        hidden_grad = r1[rows, :] * (
-            scaled
-            - jnp.mean(scaled, axis=-1, keepdims=True)
-            - unit * jnp.mean(scaled * unit, axis=-1, keepdims=True)
-        )
-        n1[rows, :] = hidden_grad
-        rounded = hidden_grad.astype(BF16)
-        ml[rows, :] = rounded
-        return (
-            sums[0] + fold8(upstream * unit), sums[1] + fold8(upstream), sums[2] + fold8(rounded.astype(F32)),
-        )
-
-    sums = lax.fori_loop(0, 15, attn_norm_back, (zero8, zero8, zero8))
-    vec[2:3, :] = jnp.sum(sums[2], axis=0, keepdims=True)
-    vec[3:4, :] = jnp.sum(sums[0], axis=0, keepdims=True)
-    vec[4:5, :] = jnp.sum(sums[1], axis=0, keepdims=True)
-    end_c(3)
-    c_s[...] = dot_nt(ml[...], wo[...]).astype(BF16)
-
-    q_rows, k_rows, v_rows = spread(q_s[0:32, :]), k_s[0:32, :], v_s[0:32, :]
-    dc_rows = spread(c_s[0:32, :])
-    soft = pq_s[...]
-    dp = dot_nt(v_rows, dc_rows)
-    soft_f = soft.astype(F32)
-    ds = (soft_f * (dp - jnp.sum(soft_f * dp, axis=0, keepdims=True))).astype(BF16)
-    v_s[0:32, :] = dot_nn(soft, dc_rows).astype(BF16)
-    k_s[0:32, :] = dot_nn(ds, q_rows).astype(BF16)
-    q_s[0:32, :] = (0.125 * gather_heads(dot_tn(ds, k_rows))).astype(BF16)
-
-    def attend_back(pair, carry):
-        lanes = pl.ds(pl.multiple_of(pair * 128, 128), 128)
+                store_grad(p, t, i, both[i])
+
+    def in_grad(p, groups):
+        at = (p - 2) * 2 * D
+        pair_grad(p, groups, mlT, gp.at[:, pl.ds(at, D)], mlT, gp.at[:, pl.ds(at + D, D)])
+
+    def inner_grad(t):
+        cols = pl.ds(t * D, D)
+        weight = wb_tile(t)
+        tmp_a[...] = dot_nt(ml[0:256, :], weight)
+        tmp_b[0:224, :] = dot_nt(ml[256:480, :], weight)
+        total = zero8
+        for ref, start, size in ((tmp_a, 0, 256), (tmp_b, 256, 224)):
+            for at, count in blocks(0, size, 16):
+                rows = pl.ds(start + at, count)
+                rounded = (ref[at:at + count, :] * gp[rows, cols].astype(F32)).astype(BF16)
+                gp[rows, cols] = rounded
+                total = total + fold8(rounded.astype(F32))
+        vec[8 + t:9 + t, :] = jnp.sum(total, axis=0, keepdims=True)
+
+    def middle_grad(t):
+        cols = pl.ds(t * D, D)
+        n2[...] += dot_nt(gp[:, cols], wi[:, cols])
+
+    def attn_norm_back():
+        sums = (zero8, zero8, zero8)
+        for at, count in blocks(0, 480, 32):
+            rows = pl.ds(at, count)
+            upstream, unit = n2[rows, :], n1[rows, :]
+            scaled = upstream * gain1
+            hidden_grad = r1[rows, :] * (
+                scaled
+                - jnp.mean(scaled, axis=-1, keepdims=True)
+                - unit * jnp.mean(scaled * unit, axis=-1, keepdims=True)
+            )
+            n1[rows, :] = hidden_grad
+            rounded = hidden_grad.astype(BF16)
+            ml[rows, :] = rounded
+            sums = (
+                sums[0] + fold8(upstream * unit), sums[1] + fold8(upstream), sums[2] + fold8(rounded.astype(F32)),
+            )
+        vec[2:3, :] = jnp.sum(sums[2], axis=0, keepdims=True)
+        vec[3:4, :] = jnp.sum(sums[0], axis=0, keepdims=True)
+        vec[4:5, :] = jnp.sum(sums[1], axis=0, keepdims=True)
+
+    def context_grad():
+        c_s[...] = dot_nt(ml[...], wo[...]).astype(BF16)
+
+    def query_slot_back():
+        q_rows, k_rows, v_rows = spread(q_s[0:32, :]), k_s[0:32, :], v_s[0:32, :]
+        dc_rows = spread(c_s[0:32, :])
+        soft = pq_s[...]
+        dp = dot_nt(v_rows, dc_rows)
+        soft_f = soft.astype(F32)
+        ds = (soft_f * (dp - jnp.sum(soft_f * dp, axis=0, keepdims=True))).astype(BF16)
+        v_s[0:32, :] = dot_nn(soft, dc_rows).astype(BF16)
+        k_s[0:32, :] = dot_nn(ds, q_rows).astype(BF16)
+        q_s[0:32, :] = (0.125 * gather_heads(dot_tn(ds, k_rows))).astype(BF16)
+
+    def attend_back(pair):
+        lanes = pl.ds(pair * 128, 128)
         for slot in range(2):
             low_at = 12 * slot
             rows = pl.ds(32 + 208 * slot, WIN)
@@ -984,72 +1035,61 @@
                     old = ref[240:256, lanes].astype(F32)
                     ref[240:256, lanes] = jnp.where(iota((16, 128), 0) >= 12, new[0:16], old).astype(BF16)
                     ref[256:480, lanes] = new[16:240].astype(BF16)
-        return carry
-
-    lax.fori_loop(0, 2, attend_back, 0)
-    end_b(0)
-    lax.fori_loop(2, 4, attend_back, 0)
-    end_a(2)
-    lax.fori_loop(4, 6, attend_back, 0)
-    end_b(1)
 
     def column_sum(ref):
-        def step(i, total):
-            return total + fold8(ref[pl.ds(pl.multiple_of(i * 16, 16), 16), :].astype(F32))
-
-        return jnp.sum(lax.fori_loop(0, 30, step, zero8), axis=0, keepdims=True)
-
-    vec[0:1, :] = column_sum(q_s)
-    vec[1:2, :] = column_sum(v_s)
-    def vec_step(i, device):
-        return remote(vec, vecr.at[i], v_send.at[i], v_recv.at[i], device)
-
-    def vec_z(hop):
-        return remote(
-            vec, vecz.at[hop - 1], v_send.at[2 + hop], v_recv.at[2 + hop], lax.rem(zz + hop, 4) * 8 + plane
-        )
-
-    vec_step(0, partner).start()
-    pair_grad(4, xT, v_s, cT, ml)
-    pair_grad(5, xT, q_s, xT, k_s)
-    vec_step(0, partner).wait()
-    vec[...] += vecr[0]
-    vec_step(1, x_peer).start()
-    end_a(3)
-    end_c(4)
-    n1[...] += dot_nt(q_s[...], wq[...])
-    end_c(5)
-    end_b(2)
-    vec_step(1, x_peer).wait()
-    vec[...] += vecr[1]
-    vec_step(2, y_peer).start()
-    n1[...] += dot_nt(k_s[...], wk[...])
-    n1[...] += dot_nt(v_s[...], wv[...])
+        total = zero8
+        for at, count in blocks(0, 480, 32):
+            total = total + fold8(ref[at:at + count, :].astype(F32))
+        return jnp.sum(total, axis=0, keepdims=True)
+
+    def column_sums():
+        vec[0:1, :] = column_sum(q_s)
+        vec[1:2, :] = column_sum(v_s)
+
+    def token_grad(grads, weight):
+        n1[...] += dot_nt(grads[...], weight[...])
+
     out_qg = pltpu.make_async_copy(n1.at[0:32, :], qtg_h, out_sem.at[2])
     out_pg = pltpu.make_async_copy(n1.at[32:472, :], ptg_h, out_sem.at[3])
-    out_qg.start()
-    out_pg.start()
-    end_z(0)
-    end_z(1)
-    vec_step(2, y_peer).wait()
-    vec[...] += vecr[2]
-    for hop in range(1, 4):
-        vec_z(hop).start()
-    end_a(4)
-    end_b(3)
-    end_z(2)
-    for hop in range(1, 4):
-        vec_z(hop).wait()
-    whole = vec[...] + vecz[0] + vecz[1] + vecz[2]
-    small_o[0:8, :] = pltpu.roll(whole[0:8], D - 24 * me, 1)[:, 0:128]
-    wide = pltpu.roll(whole[8:16], D - 96 * plane, 1)
-    small_o[8:9, :] = jnp.sum(jnp.where(iota((8, D), 0) == zz, wide, 0.0), axis=0, keepdims=True)[:, 0:128]
-    end_a(5)
-    end_b(4)
-    end_z(3)
-    end_b(5)
-    end_z(4)
-    end_z(5)
+
+    def send_tokens():
+        out_qg.start()
+        out_pg.start()
+
+    def vec_step(i):
+        return remote(vec, vecr.at[i], v_send.at[i], v_recv.at[i], (partner, x_peer, y_peer)[i])
+
+    def vec_z():
+        return [
+            remote(vec, vecz.at[hop - 1], v_send.at[2 + hop], v_recv.at[2 + hop], lax.rem(zz + hop, 4) * 8 + plane)
+            for hop in range(1, 4)
+        ]
+
+    def vec_on(i):
+        if i > 0:
+            vec_step(i - 1).wait()
+            vec[...] += vecr[i - 1]
+        begin([vec_step(i)] if i < 3 else vec_z())
+
+    def vec_end():
+        finish_steps(vec_z())
+        whole = vec[...] + vecz[0] + vecz[1] + vecz[2]
+        small_o[0:8, :] = pltpu.roll(whole[0:8], D - 24 * me, 1)[:, 0:128]
+        wide = pltpu.roll(whole[8:16], D - 96 * plane, 1)
+        small_o[8:9, :] = jnp.sum(jnp.where(iota((8, D), 0) == zz, wide, 0.0), axis=0, keepdims=True)[:, 0:128]
+
+    pieces_of = {
+        "wback": back_grad, "dinner": inner_grad, "win": in_grad, "dmid": middle_grad, "lnback": attn_norm_back,
+        "dctx": context_grad, "qslot": query_slot_back, "attn": attend_back, "sums": column_sums,
+        "wvo": lambda groups: pair_grad(4, groups, xT, v_s, cT, ml),
+        "wqk": lambda groups: pair_grad(5, groups, xT, q_s, xT, k_s),
+        "tq": lambda: token_grad(q_s, wq), "tk": lambda: token_grad(k_s, wk), "tv": lambda: token_grad(v_s, wv),
+        "tout": send_tokens, "vec": vec_on, "vecend": vec_end,
+        "c": start_c, "ec": end_c, "e1": end_1, "e2": end_2, "e3": end_3,
+    }
+    for name, *operands in ORDER:
+        pieces_of[name](*operands)
+
     out_q.wait()
     out_p.wait()
     out_qg.wait()
@@ -1096,10 +1136,11 @@
         ),
         in_specs=[
             hbm, hbm, smem, smem, smem, smem, smem, smem, hbm, hbm,
-            hbm, vmem, hbm, hbm, vmem, hbm, vmem, vmem, vmem, hbm, vmem, hbm, vmem, vmem, vmem,
+            *(hbm,) * 15,
         ],
         out_specs=(hbm,) * 4 + (vmem,) * 7,
         scratch_shapes=[
+            *(pltpu.VMEM((size,), BF16) for size in (D, D, D, D, D, FF, D, D, D)),
             pltpu.VMEM((D, D), BF16), pltpu.VMEM((D, D), BF16), pltpu.VMEM((D, D), BF16), pltpu.VMEM((D, D), BF16),
             pltpu.VMEM((D, FF), BF16), pltpu.VMEM((2, 2, 2, 4, 2, 2, 48, 384), BF16),
             pltpu.VMEM((440, D), BF16), pltpu.VMEM((ROWS, D), BF16), pltpu.VMEM((D, ROWS), BF16),
@@ -1108,7 +1149,8 @@
             pltpu.VMEM((ROWS, D), BF16), pltpu.VMEM((D, ROWS), BF16),
             pltpu.VMEM((ROWS, D), F32), pltpu.VMEM((ROWS, D), F32), pltpu.VMEM((ROWS, 1), F32), pltpu.VMEM((ROWS, 1), F32),
             pltpu.VMEM((ROWS, D), BF16), pltpu.VMEM((D, ROWS), BF16),
-            pltpu.VMEM((ROWS, D), BF16), pltpu.VMEM((FF, ROWS), BF16), pltpu.VMEM((ROWS, D), F32),
+            pltpu.VMEM((256, D), BF16), pltpu.VMEM((256, D), BF16), pltpu.VMEM((FF, ROWS), BF16),
+            pltpu.VMEM((256, D), F32), pltpu.VMEM((256, D), F32),
             pltpu.VMEM((ROWS, FF), BF16),
             pltpu.VMEM((32, D), BF16), pltpu.VMEM((440, D), BF16), pltpu.VMEM((32, D), BF16), pltpu.VMEM((440, D), BF16),
             pltpu.VMEM((768, 128), F32), pltpu.VMEM((8, D), F32),
@@ -1116,14 +1158,15 @@
             pltpu.VMEM((4, 2, 2, 4, 2, 2, 48, 384), BF16),
             pltpu.VMEM((2, 2, 4, 2, 2, 48, 384), BF16), pltpu.VMEM((6, 2, 4, 2, 48, 384), BF16),
             pltpu.VMEM((6, 2, 4, 48, 384), BF16), pltpu.VMEM((6, 2, 3, 48, 384), BF16),
-            pltpu.SemaphoreType.DMA((12,)), pltpu.SemaphoreType.DMA((4,)),
+            pltpu.VMEM((3, 2, 2, 48, 384), BF16),
+            pltpu.SemaphoreType.DMA((24,)), pltpu.SemaphoreType.DMA((4,)),
             pltpu.SemaphoreType.DMA((16,)), pltpu.SemaphoreType.DMA((16,)),
             pltpu.SemaphoreType.DMA((6, 2)), pltpu.SemaphoreType.DMA((6, 2)),
             pltpu.SemaphoreType.DMA((6, 2)), pltpu.SemaphoreType.DMA((6, 2)),
             pltpu.SemaphoreType.DMA((6, 2)), pltpu.SemaphoreType.DMA((6, 2)),
             pltpu.SemaphoreType.DMA((6, 2, 3)), pltpu.SemaphoreType.DMA((6, 2, 3)),
             pltpu.SemaphoreType.DMA((6,)), pltpu.SemaphoreType.DMA((6,)),
-            pltpu.SemaphoreType.REGULAR,
+            pltpu.SemaphoreType.REGULAR((2, 2)),
         ],
         compiler_params=pltpu.CompilerParams(
             collective_id=0, has_side_effects=True, vmem_limit_bytes=64 * 1024 * 1024 - 65536,

time: 131 us -> 111 us (0.85)
  Pallas kernels: 127 us -> 107 us
    pallas_call x1, Pallas kernels: 123 us -> 103 us  [on_device_small(): pl.pallas_call(layer_kernel, out_shape=(*large, shape((16, 128), F32)), i...]
where the time goes in v3:
time: 111 us
  Pallas kernels  107 us (96%)
  between operations  3.45 us (3%)
    pallas_call x1, Pallas kernels, on_device_small(): pl.pallas_call(layer_kernel, out_shape=(*large, shape((16, 128), F32)), i...  103 us
    pallas_call x1, Pallas kernels, on_device_small(): pl.pallas_call(hand_on_kernel, out_shape=large + (shape((24,), F32),) * 8...  4.42 us

profile of v3, /device:TPU:0, one launch (start us, length us, event | category | flops | bytes accessed | tf_op | source)
XLA Modules:
  0.0 110.9 jit_solution(16868519830342976828)
XLA Ops:
  3.2 103.0 %encoder_layer.1 = (bf16[32,768]{1,0:T(8,128)(2,1)}, bf16[440,768]{1,0:T(8,128)(2,1)}, f32[32,768]{1,0:T(8,128)}, f32[440,768]{1,0:T(8,128)}, f32[24,768]{1,0:T(...) custom-call(bf16[32,768]{1,0:T(8,128)(2,1)} %qtok.1, ...), custom_call_target="tpu_custom_call" | custom-call | tf_op jit(solution)/shard_map/encoder_layer/pallas_call | solution.py:1132
  106.3 4.4 %hand_on.1 = (bf16[32,768]{1,0:T(8,128)(2,1)}, bf16[440,768]{1,0:T(8,128)(2,1)}, f32[32,768]{1,0:T(8,128)}, f32[440,768]{1,0:T(8,128)}, f32[24,768]{1,0:T(8,128)...) custom-call(bf16[32,768]{1,0:T(8,128)(2,1)} %get-tuple-element.51.re, ...), custom_call_target="tpu_custom_call" | custom-call | tf_op jit(solution)/shard_map/hand_on/pallas_call | solution.py:1181
